TPU v7x, 512 devices: a whole 4x8x8 slice. The times are simulated.
512 devices in a mesh: band: 8 (over z), pw: 64 (over y, x, core).
Axes of the slice: x: 4, y: 8, z: 8, core: 2. Of those that a mesh axis runs over, the one named last changes fastest.
Arguments:
- basis_re: float32 [8, 8, 8, 16384], P(None, None, 'band', 'pw'), may hold values from -24 to 24
- basis_im: float32 [8, 8, 8, 16384], P(None, None, 'band', 'pw'), may hold values from -24 to 24
- potential: float32 [192, 192, 192], P('pw'), may hold values from -15 to 15
- kinetic: float32 [8, 16384], P(None, 'pw'), may hold values from 0 to 30
- form_factors: float32 [8, 8, 16384], P(None, None, 'pw'), may hold values from -12 to 12
- channel_strength: float32 [8], replicated, may hold values from -4 to 4
- sphere_map: int32 [8, 16384], P(None, 'pw'), may hold values from 0 to 6143, as said below
- column_map: int32 [2048], replicated, may hold values from 0 to 36863, as said below
- atom_sites: int32 [3, 512], replicated, may hold values from 0 to 191
Outputs:
- next_re: float32 [8, 8, 16384], P(None, 'band', 'pw')
- next_im: float32 [8, 8, 16384], P(None, 'band', 'pw')
- coeffs_re: float32 [8, 8, 8], replicated
- coeffs_im: float32 [8, 8, 8], replicated
- chol_re: float32 [8, 8], replicated
- chol_im: float32 [8, 8], replicated
Inputs may be any that keep to these rules, and one draw needn't show every extreme that they name: `sphere_map`: within each group of 256 consecutive values of the second index, the entries over both indices are distinct. `column_map`: all entries are distinct.
All inputs are finite; a program needn't handle non-finite values.
Results may differ from a plain program's by a relative error of at most 0.0015.
The roundings to bfloat16 on the way count: a program that leaves them out, or rounds other values in their place, can miss the bound.
Values sent between devices are 32-bit elements; how exact they have to be, the bound alone decides.
No kernel may reach another device: no remote copies, remote signals or barrier semaphores. Data moves between devices by JAX's collectives and lax.ppermute only.
A program may use at most 128 MiB of HBM per device.

v0:
```python
import math

import jax
import jax.numpy as jnp
from jax import lax
from jax.sharding import PartitionSpec as P

exact_mode = lax.Precision.HIGHEST


def contract(left, right, left_dim, right_dim):
    return lax.dot_general(
        left,
        right,
        (((left_dim,), (right_dim,)), ((), ())),
        precision=exact_mode,
        preferred_element_type=jnp.float32,
    )


def conj_product(left_re, left_im, right_re, right_im, left_dim, scale):
    real = contract(left_re, right_re, left_dim, left_dim) + contract(
        left_im, right_im, left_dim, left_dim
    )
    imag = contract(left_re, right_im, left_dim, left_dim) - contract(
        left_im, right_re, left_dim, left_dim
    )
    return (real * scale, imag * scale)


def dft_tables(length, sign, scale):
    ticks = jnp.arange(length, dtype=jnp.int32)
    turns = ticks[:, None] * ticks[None, :] % length
    angle = turns.astype(jnp.float32) * (2.0 * math.pi / length)
    return (jnp.cos(angle) * scale, sign * jnp.sin(angle) * scale)


def along_depth(cos_table, sin_table, part_re, part_im):

    def apply(table, part):
        return jnp.einsum("pz,bzc->bpc", table, part, precision=exact_mode)

    return (
        apply(cos_table, part_re) - apply(sin_table, part_im),
        apply(sin_table, part_re) + apply(cos_table, part_im),
    )


def along_rows(joint, cos_table, sin_table):
    matrix = jnp.concatenate(
        [jnp.concatenate([cos_table, sin_table], 1), jnp.concatenate([-sin_table, cos_table], 1)], 0
    )
    return jnp.matmul(joint, matrix, precision=exact_mode)


def along_x(joint, cos_table, sin_table):
    width = cos_table.shape[0]
    stacked = jnp.concatenate([cos_table, sin_table], 0)
    mixed = jnp.einsum("px,kzxy->kzpy", stacked, joint, precision=exact_mode)
    upper = mixed[:, :, :width]
    lower = mixed[:, :, width:]
    out_re = upper[..., :width] - lower[..., width:]
    out_im = upper[..., width:] + lower[..., :width]
    return jnp.concatenate([out_re, out_im], 3)


def phase_table(depth, x_index, y_index, atom_sites, grid):
    turns = (
        depth[:, None] * atom_sites[0][None, :]
        + x_index[:, None] * atom_sites[1][None, :]
        + y_index[:, None] * atom_sites[2][None, :]
    ) % grid
    angle = turns.astype(jnp.float32) * (2.0 * math.pi / grid)
    return jnp.concatenate(
        [jnp.cos(angle).astype(jnp.bfloat16), jnp.sin(angle).astype(jnp.bfloat16)], 1
    )


def weigh(form, wave_re, wave_im):
    channels = form.shape[0]
    bands = wave_re.shape[0]
    part_re = (form[:, None, :] * wave_re[None]).reshape(channels * bands, -1)
    part_im = (form[:, None, :] * wave_im[None]).reshape(channels * bands, -1)
    return jnp.concatenate([part_re.astype(jnp.bfloat16), part_im.astype(jnp.bfloat16)], 0)


def project(weighted, phase):
    half = weighted.shape[0] // 2
    atoms = phase.shape[1] // 2
    mixed = jnp.dot(weighted, phase, preferred_element_type=jnp.float32)
    return (
        mixed[:half, :atoms] - mixed[half:, atoms:],
        mixed[:half, atoms:] + mixed[half:, :atoms],
    )


def apply_back(form, sum_re, sum_im, strength, phase, root_waves):
    channels = form.shape[0]
    bands = sum_re.shape[0] // channels
    factor = jnp.repeat(strength, bands)[:, None]
    scaled_re = (factor * (sum_re / root_waves) / root_waves).astype(jnp.bfloat16)
    scaled_im = (factor * (sum_im / root_waves) / root_waves).astype(jnp.bfloat16)
    stacked = jnp.concatenate(
        [jnp.concatenate([scaled_re, scaled_im], 1), jnp.concatenate([scaled_im, -scaled_re], 1)], 0
    )
    mixed = lax.dot_general(
        stacked, phase, (((1,), (1,)), ((), ())), preferred_element_type=jnp.float32
    )
    back_re = mixed[: channels * bands].reshape(channels, bands, -1)
    back_im = mixed[channels * bands :].reshape(channels, bands, -1)
    return (jnp.sum(form[:, None, :] * back_re, 0), jnp.sum(form[:, None, :] * back_im, 0))


def subtract_span(image_re, image_im, flat_re, flat_im, coef_re, coef_im):
    span_re = contract(coef_re, flat_re, 0, 0) - contract(coef_im, flat_im, 0, 0)
    span_im = contract(coef_re, flat_im, 0, 0) + contract(coef_im, flat_re, 0, 0)
    return (image_re - span_re, image_im - span_im)


def combine_rows(solved_re, solved_im, wave_re, wave_im):
    out_re = contract(solved_re, wave_re, 0, 0) - contract(solved_im, wave_im, 0, 0)
    out_im = contract(solved_re, wave_im, 0, 0) + contract(solved_im, wave_re, 0, 0)
    return (out_re, out_im)


def cholesky_upper(gram_re, gram_im):
    size = gram_re.shape[0]
    ticks = jnp.arange(size)

    def cholesky_one_row(row_index, carry):
        upper_re, upper_im = carry
        column_re = upper_re[:, row_index]
        column_im = upper_im[:, row_index]
        total_re = gram_re[row_index] - (
            jnp.dot(column_re, upper_re, precision=exact_mode)
            + jnp.dot(column_im, upper_im, precision=exact_mode)
        )
        total_im = gram_im[row_index] - (
            jnp.dot(column_re, upper_im, precision=exact_mode)
            - jnp.dot(column_im, upper_re, precision=exact_mode)
        )
        pivot = jnp.sqrt(total_re[row_index])
        new_re = jnp.where(ticks >= row_index, total_re / pivot, 0.0)
        new_im = jnp.where(ticks > row_index, total_im / pivot, 0.0)
        return (upper_re.at[row_index].set(new_re), upper_im.at[row_index].set(new_im))

    zero = jnp.zeros((size, size), gram_re.dtype)
    return lax.fori_loop(0, size, cholesky_one_row, (zero, zero))


def invert_upper(upper_re, upper_im):
    size = upper_re.shape[0]
    identity = jnp.eye(size, dtype=upper_re.dtype)

    def invert_one_row(step_index, carry):
        solved_re, solved_im = carry
        row_index = size - 1 - step_index
        lead_re = upper_re[row_index]
        lead_im = upper_im[row_index]
        right_re = identity[row_index] - (
            jnp.dot(lead_re, solved_re, precision=exact_mode)
            - jnp.dot(lead_im, solved_im, precision=exact_mode)
        )
        right_im = -(
            jnp.dot(lead_re, solved_im, precision=exact_mode)
            + jnp.dot(lead_im, solved_re, precision=exact_mode)
        )
        pivot = upper_re[row_index, row_index]
        return (
            solved_re.at[row_index].set(right_re / pivot),
            solved_im.at[row_index].set(right_im / pivot),
        )

    zero = jnp.zeros((size, size), upper_re.dtype)
    return lax.fori_loop(0, size, invert_one_row, (zero, zero))


def body(
    basis_re,
    basis_im,
    potential,
    kinetic,
    form_factors,
    channel_strength,
    sphere_map,
    column_map,
    atom_sites,
):
    blocks, slab, single, row_count = basis_re.shape
    band_count = lax.axis_size("band")
    wave_groups = lax.axis_size("pw")
    planes, grid, width = potential.shape
    column_count = column_map.shape[0] // wave_groups
    total_waves = band_count * wave_groups * row_count
    root_waves = math.sqrt(total_waves)
    inverse_cos, inverse_sin = dft_tables(grid, 1.0, 1.0 / grid)
    forward_cos, forward_sin = dft_tables(grid, -1.0, 1.0)
    flat_re = basis_re.reshape(blocks * slab, row_count)
    flat_im = basis_im.reshape(blocks * slab, row_count)
    current_re = basis_re[blocks - 1]
    current_im = basis_im[blocks - 1]
    band_re, band_im = (
        lax.all_to_all(current_re, "band", split_axis=0, concat_axis=1, tiled=True),
        lax.all_to_all(current_im, "band", split_axis=0, concat_axis=1, tiled=True),
    )
    band_dev = band_re.shape[0]
    psi_re = band_re.reshape(band_dev, -1)
    psi_im = band_im.reshape(band_dev, -1)
    cells = sphere_map.reshape(-1)
    depth = cells // column_count
    plane_pos = column_map[lax.axis_index("pw") * column_count + cells % column_count]
    x_index = plane_pos // grid
    y_index = plane_pos % grid
    form_flat = form_factors.reshape(form_factors.shape[0], -1)
    phase = phase_table(depth, x_index, y_index, atom_sites, grid)
    part_re, part_im = project(weigh(form_flat, psi_re, psi_im), phase)
    sum_re, sum_im = lax.psum((part_re, part_im), "pw")
    near_re, near_im = apply_back(form_flat, sum_re, sum_im, channel_strength, phase, root_waves)
    doubled = jnp.concatenate([potential, potential], 2)
    empty_columns = jnp.zeros((band_dev, grid * column_count), jnp.float32)
    column_re = empty_columns.at[:, cells].set(psi_re).reshape(band_dev, grid, column_count)
    column_im = empty_columns.at[:, cells].set(psi_im).reshape(band_dev, grid, column_count)
    column_re, column_im = along_depth(inverse_cos, inverse_sin, column_re, column_im)
    part_re = lax.all_to_all(column_re, "pw", split_axis=1, concat_axis=2, tiled=True)
    part_im = lax.all_to_all(column_im, "pw", split_axis=1, concat_axis=2, tiled=True)
    count = part_re.shape[0]
    empty = jnp.zeros((count, planes, grid * grid), jnp.float32)
    plane_re = empty.at[:, :, column_map].set(part_re).reshape(count, planes, grid, grid)
    plane_im = empty.at[:, :, column_map].set(part_im).reshape(count, planes, grid, grid)
    joint = jnp.concatenate([plane_re, plane_im], 3)
    joint = along_x(along_rows(joint, inverse_cos, inverse_sin), inverse_cos, inverse_sin)
    joint = joint * doubled[None]
    joint = along_rows(along_x(joint, forward_cos, forward_sin), forward_cos, forward_sin)
    out_re = joint[:, :, :, :grid].reshape(count, planes, grid * grid)[:, :, column_map]
    out_im = joint[:, :, :, grid:].reshape(count, planes, grid * grid)[:, :, column_map]
    back_re = lax.all_to_all(out_re, "pw", split_axis=2, concat_axis=1, tiled=True)
    back_im = lax.all_to_all(out_im, "pw", split_axis=2, concat_axis=1, tiled=True)
    back_re, back_im = along_depth(forward_cos, forward_sin, back_re, back_im)
    local_re = back_re.reshape(band_dev, -1)[:, cells]
    local_im = back_im.reshape(band_dev, -1)[:, cells]
    kinetic_flat = kinetic.reshape(-1)
    image_re = kinetic_flat * psi_re + local_re
    image_im = kinetic_flat * psi_im + local_im
    image_re = image_re + near_re
    image_im = image_im + near_im
    row_re, row_im = (
        lax.all_to_all(
            image_re.reshape(band_dev, band_count, row_count),
            "band",
            split_axis=1,
            concat_axis=0,
            tiled=True,
        ),
        lax.all_to_all(
            image_im.reshape(band_dev, band_count, row_count),
            "band",
            split_axis=1,
            concat_axis=0,
            tiled=True,
        ),
    )
    row_re = row_re[:, 0, :]
    row_im = row_im[:, 0, :]
    part_re, part_im = conj_product(flat_re, flat_im, row_re, row_im, 1, 1.0 / total_waves)
    coef_re, coef_im = lax.psum((part_re, part_im), ("band", "pw"))
    res_re, res_im = subtract_span(row_re, row_im, flat_re, flat_im, coef_re, coef_im)
    gram_re, gram_im = conj_product(res_re, res_im, res_re, res_im, 1, 1.0 / total_waves)
    gram_re, gram_im = lax.psum((gram_re, gram_im), ("band", "pw"))
    upper_re, upper_im = cholesky_upper(gram_re, gram_im)
    solved_re, solved_im = invert_upper(upper_re, upper_im)
    next_re, next_im = combine_rows(solved_re, solved_im, res_re, res_im)
    return (
        next_re.reshape(slab, 1, row_count),
        next_im.reshape(slab, 1, row_count),
        coef_re.reshape(blocks, slab, slab),
        coef_im.reshape(blocks, slab, slab),
        upper_re,
        upper_im,
    )


def solution(mesh):
    return jax.shard_map(
        body,
        mesh=mesh,
        in_specs=(
            P(None, None, "band", "pw"),
            P(None, None, "band", "pw"),
            P("pw", None, None),
            P(None, "pw"),
            P(None, None, "pw"),
            P(),
            P(None, "pw"),
            P(),
            P(),
        ),
        out_specs=(P(None, "band", "pw"), P(None, "band", "pw"), P(), P(), P(), P()),
        check_vma=False,
    )
```

profile of v0, /device:TPU:1, one launch (start us, length us, event | category | flops | bytes accessed | tf_op | source)
XLA Modules:
  0.0 838.9 jit_solution(13010280401035136830)
XLA Ops:
  1.9 10.9 %all-to-all-start = ((f32[8,1,256]{2,1,0:T(1,128)}), f32[8,1,256]{2,1,0:T(1,128)S(1)}, u32[]{:S(2)}, u32[]{:S(2)}) async-start(f32[8,1,256]{2,1,0:T(1,128)} %slice_bitcast_fusion.1), calls=%async_computation | async-start | bytes 16384 | tf_op jit(solution)/shard_map/all_to_all | solution.py:203
  19.2 11.8 %gather_fusion.3 = s32[2048]{0:T(1024)S(1)} fusion(s32[2048]{0:T(1024)S(1)} %copy-done, s32[2048]{0:T(1024)S(1)} %broadcast_clamp_fusion), kind=kCustom, calls=%fused_computation.3 | custom fusion | bytes 24576 | tf_op jit(solution)/shard_map/gather | solution.py:211
  31.6 20.4 %cosine_convert_fusion = (bf16[2048,512]{1,0:T(8,128)(2,1)S(1)}, bf16[2048,512]{1,0:T(8,128)(2,1)}) fusion(s32[512]{0:T(512)S(1)} %bitcast.400, s32[2048]{0:T(1024)S(1)} %get-tuple-element.474, s32[512]{0:T(512)S(1)} %bitcast.401, s32[2048]{0:T(1024)S(1)} %get-tuple-element.473, s32[512]{0:T(512)S(1)} %bitcast.399, s32[2048]{0:T(1024)S(1)} %get-tuple-element.475), kind=kLoop, calls=%fused_computation.70 | loop fusion | flops 15728640 | bytes 4225024 | tf_op jit(solution)/shard_map/convert_element_type | solution.py:75
  52.8 6.7 all-to-all-start.1
  59.4 8.1 scatter_custom_fusion
  71.5 8.2 scatter_custom_fusion.1
  82.4 11.6 %all-to-all-start.2 = ((f32[1,192,32]{2,0,1:T(1,128)}), f32[1,192,32]{2,0,1:T(1,128)S(1)}, u32[]{:S(2)}, u32[]{:S(2)}) async-start(f32[1,192,32]{2,0,1:T(1,128)} %copy.63), calls=%async_computation.2 | async-start | bytes 196608 | tf_op jit(solution)/shard_map/all_to_all | solution.py:224
  97.6 245.9 %all-reduce.2 = (f32[8,512]{1,0:T(8,128)}, f32[8,512]{1,0:T(8,128)}) all-reduce(f32[8,512]{1,0:T(8,128)} %get-tuple-element.459, f32[8,512]{1,0:T(8,128)} %get-tuple-element.458), channel_id=1, replica_groups=mesh['band'=8,'pw'=64] {'pw'}, use_global_device_ids=true, to_apply=%region_4.5 | all-reduce | flops 8192 | bytes 65536 | tf_op jit(solution)/shard_map/psum | solution.py:217
  350.2 11.6 %all-to-all-start.3 = ((f32[1,192,32]{2,0,1:T(1,128)}), f32[1,192,32]{2,0,1:T(1,128)S(1)}, u32[]{:S(2)}, u32[]{:S(2)}) async-start(f32[1,192,32]{2,0,1:T(1,128)} %copy.67), calls=%async_computation.3 | async-start | bytes 196608 | tf_op jit(solution)/shard_map/all_to_all | solution.py:225
  361.9 3.5 fusion.43
  365.9 13.4 %scatter_custom_fusion.2 = f32[3,36864]{0,1:T(8,128)} fusion(s32[2048]{0:T(1024)} %get-tuple-element.467, f32[2048,3]{1,0:T(8,128)S(1)} %copy.65, f32[]{:T(128)} %constant.311.clone.1), kind=kCustom, calls=%fused_computation.63 | custom fusion | bytes 442880 | tf_op jit(solution)/shard_map/scatter | solution.py:228
  379.2 11.7 %copy.89 = f32[1,3,192,192]{3,2,1,0:T(8,128)S(1)} copy(f32[1,3,192,192]{1,3,2,0:T(8,128)} %bitcast.371) | data formatting | bytes 884736 | tf_op jit(solution)/shard_map/reshape | solution.py:228
  391.5 13.5 %scatter_custom_fusion.3 = f32[3,36864]{0,1:T(8,128)} fusion(s32[2048]{0:T(1024)} %get-tuple-element.467, f32[2048,3]{1,0:T(8,128)S(1)} %copy.69, f32[]{:T(128)} %constant.311.clone.1), kind=kCustom, calls=%fused_computation.61 | custom fusion | bytes 442880 | tf_op jit(solution)/shard_map/scatter | solution.py:229
  405.0 11.7 %copy.90 = f32[1,3,192,192]{3,2,1,0:T(8,128)S(1)} copy(f32[1,3,192,192]{1,3,2,0:T(8,128)} %bitcast.370) | data formatting | bytes 884736 | tf_op jit(solution)/shard_map/reshape | solution.py:229
  425.4 9.6 %copy.93 = f32[1,3,192,192]{1,3,2,0:T(8,128)} copy(f32[1,3,192,192]{3,2,1,0:T(8,128)S(1)} %get-tuple-element.457) | data formatting | bytes 884736 | tf_op jit(solution)/shard_map/reshape | solution.py:234
  435.0 14.0 %gather_fusion = f32[2048,3]{1,0:T(8,128)} fusion(f32[3,36864]{0,1:T(8,128)} %bitcast.372, s32[2048]{0:T(1024)S(1)} %get-tuple-element.466), kind=kCustom, calls=%fused_computation | custom fusion | bytes 57344 | tf_op jit(solution)/shard_map/gather | solution.py:234
  449.0 10.3 %all-to-all-start.4 = ((f32[1,3,2048]{1,0,2:T(1,128)}), f32[1,3,2048]{1,0,2:T(1,128)S(1)}, u32[]{:S(2)}, u32[]{:S(2)}) async-start(f32[1,3,2048]{1,0,2:T(1,128)} %bitcast.50), calls=%async_computation.4 | async-start | bytes 2097152 | tf_op jit(solution)/shard_map/all_to_all | solution.py:236
  459.4 9.6 %copy.94 = f32[1,3,192,192]{1,3,2,0:T(8,128)} copy(f32[1,3,192,192]{3,2,1,0:T(8,128)S(1)} %get-tuple-element.456) | data formatting | bytes 884736 | tf_op jit(solution)/shard_map/reshape | solution.py:235
  469.0 14.0 %gather_fusion.1 = f32[2048,3]{1,0:T(8,128)} fusion(f32[3,36864]{0,1:T(8,128)} %bitcast.373, s32[2048]{0:T(1024)S(1)} %get-tuple-element.466), kind=kCustom, calls=%fused_computation.1 | custom fusion | bytes 57344 | tf_op jit(solution)/shard_map/gather | solution.py:235
  483.0 4.3 all-to-all-done.4
  487.3 6.5 all-to-all-start.5
  496.4 25.4 %all-to-all-done.5 = f32[1,3,2048]{1,0,2:T(1,128)S(1)} async-done(((f32[1,3,2048]{1,0,2:T(1,128)}), f32[1,3,2048]{1,0,2:T(1,128)S(1)}, u32[]{:S(2)}, u32[]{:S(2)}) %all-to-all-start.5) | async-done | bytes 24608 | tf_op jit(solution)/shard_map/all_to_all | solution.py:237
  523.5 11.8 %gather_fusion.2 = f32[2048]{0:T(1024)S(1)} fusion(f32[6144]{0:T(1024)S(1)} %reshape.602, s32[2048]{0:T(1024)S(1)} %copy-done.9), kind=kCustom, calls=%fused_computation.2 | custom fusion | bytes 24576 | tf_op jit(solution)/shard_map/gather | solution.py:239
  536.6 11.8 %gather_fusion.4 = f32[2048]{0:T(1024)S(1)} fusion(f32[6144]{0:T(1024)S(1)} %reshape.620, s32[2048]{0:T(1024)S(1)} %copy-done.9), kind=kCustom, calls=%fused_computation.4 | custom fusion | bytes 24576 | tf_op jit(solution)/shard_map/gather | solution.py:240
  549.1 6.9 all-to-all-start.7
  556.6 6.0 all-to-all-done.7
  562.6 3.3 all-to-all-start.6
  566.1 6.4 all-to-all-done.6
  572.9 97.3 %all-reduce.1 = (f32[64,8]{0,1:T(8,128)S(1)}, f32[64,8]{0,1:T(8,128)S(1)}) all-reduce(f32[64,8]{0,1:T(8,128)S(1)} %fusion.58, f32[64,8]{0,1:T(8,128)S(1)} %fusion.56), channel_id=1, replica_groups=mesh['band'=8,'pw'=64] {'band','pw'}, use_global_device_ids=true, to_apply=%region_8.9 | all-reduce | flops 1024 | bytes 8192 | tf_op jit(solution)/shard_map/psum | solution.py:265
  671.3 94.5 %all-reduce = (f32[8,8]{1,0:T(8,128)S(1)}, f32[8,8]{1,0:T(8,128)S(1)}) all-reduce(f32[8,8]{1,0:T(8,128)S(1)} %fusion.54, f32[8,8]{1,0:T(8,128)S(1)} %fusion.53), channel_id=1, replica_groups=mesh['band'=8,'pw'=64] {'band','pw'}, use_global_device_ids=true, to_apply=%region_10.11 | all-reduce | flops 128 | bytes 1024 | tf_op jit(solution)/shard_map/psum | solution.py:268
  765.8 33.1 %while.39 = (s32[]{:T(128)}, f32[8,8]{1,0:T(8,128)S(1)}, f32[8,8]{1,0:T(8,128)S(1)}, f32[8,8]{1,0:T(8,128)S(1)}, f32[8,8]{1,0:T(8,128)S(1)}, /*index=5*/s32[]{:T(128)}, s32[2]{0:T(128)S(1)}, s32[1]{0:T(128)}, s32[]{:T(128)}) while((s32[]{:T(128)}, f32[8,8]{1,0:T(8,128)S(1)}, f32[8,8]{1,0:T(8,128)S(1)}, ...), condition=%wide.region_14.15_spmd.clone.clone, body=%wide.region_12.14_spmd.clone.clone.sunk | while | flops 3179 | bytes 11794 | solution.py:148
  799.0 36.0 %while.38 = (s32[]{:T(128)}, f32[8,8]{1,0:T(8,128)S(1)}, f32[8,8]{1,0:T(8,128)S(1)}, f32[8,8]{1,0:T(8,128)S(1)}, f32[8,8]{1,0:T(8,128)S(1)}, /*index=5*/f32[8,8]...) while((s32[]{:T(128)}, f32[8,8]{1,0:T(8,128)S(1)}, ...), condition=%wide.region_17.18_spmd, body=%wide.region_15.17_spmd.sunk | while | flops 3151 | bytes 25552 | solution.py:175
  (267 shorter events, 110.7 us)
Async XLA Ops:
  0.6 18.6 %copy-start = (s32[2048]{0:T(1024)S(1)}, s32[2048]{0:T(1024)}, u32[]{:S(2)}) copy-start(s32[2048]{0:T(1024)} %param.28) | copy-start | bytes 24580
  1.9 50.8 %all-to-all-start = ((f32[8,1,256]{2,1,0:T(1,128)}), f32[8,1,256]{2,1,0:T(1,128)S(1)}, u32[]{:S(2)}, u32[]{:S(2)}) async-start(f32[8,1,256]{2,1,0:T(1,128)} %slice_bitcast_fusion.1), calls=%async_computation | async-start | bytes 16384 | tf_op jit(solution)/shard_map/all_to_all | solution.py:203
  19.2 11.8 %copy-start.12 = (s32[8,256]{1,0:T(8,128)S(1)}, s32[8,256]{1,0:T(8,128)}, u32[]{:S(2)}) copy-start(s32[8,256]{1,0:T(8,128)} %param.27) | copy-start | bytes 24580
  19.2 11.9 %copy-start.14 = (s32[3,512]{1,0:T(4,128)S(1)}, s32[3,512]{1,0:T(4,128)}, u32[]{:S(2)}) copy-start(s32[3,512]{1,0:T(4,128)} %param.29) | copy-start | bytes 18436
  19.2 11.9 %copy-start.15 = (f32[8]{0:T(128)S(1)}, f32[8]{0:T(128)}, u32[]{:S(2)}) copy-start(f32[8]{0:T(128)} %param.26) | copy-start | bytes 100
  31.0 21.7 %copy-start.10 = (f32[8,8,256]{2,1,0:T(8,128)S(1)}, f32[8,8,256]{2,1,0:T(8,128)}, u32[]{:S(2)}) copy-start(f32[8,8,256]{2,1,0:T(8,128)} %param.25) | copy-start | bytes 196612
  52.8 18.2 %all-to-all-start.1 = ((f32[8,1,256]{2,1,0:T(1,128)}), f32[8,1,256]{2,1,0:T(1,128)S(1)}, u32[]{:S(2)}, u32[]{:S(2)}) async-start(f32[8,1,256]{2,1,0:T(1,128)} %slice_bitcast_fusion), calls=%async_computation.1 | async-start | bytes 16384 | tf_op jit(solution)/shard_map/all_to_all | solution.py:204
  70.9 0.6 copy-start.7
  82.4 267.8 %all-to-all-start.2 = ((f32[1,192,32]{2,0,1:T(1,128)}), f32[1,192,32]{2,0,1:T(1,128)S(1)}, u32[]{:S(2)}, u32[]{:S(2)}) async-start(f32[1,192,32]{2,0,1:T(1,128)} %copy.63), calls=%async_computation.2 | async-start | bytes 196608 | tf_op jit(solution)/shard_map/all_to_all | solution.py:224
  350.2 40.7 %all-to-all-start.3 = ((f32[1,192,32]{2,0,1:T(1,128)}), f32[1,192,32]{2,0,1:T(1,128)S(1)}, u32[]{:S(2)}, u32[]{:S(2)}) async-start(f32[1,192,32]{2,0,1:T(1,128)} %copy.67), calls=%async_computation.3 | async-start | bytes 196608 | tf_op jit(solution)/shard_map/all_to_all | solution.py:225
  416.7 4.1 copy-start.5
  425.4 33.9 %copy-start.6 = (f32[16,2048]{1,0:T(8,128)S(1)}, f32[16,2048]{1,0:T(8,128)}, u32[]{:S(2)}) copy-start(f32[16,2048]{1,0:T(8,128)} %fusion.43) | copy-start | bytes 393220
  449.0 38.3 %all-to-all-start.4 = ((f32[1,3,2048]{1,0,2:T(1,128)}), f32[1,3,2048]{1,0,2:T(1,128)S(1)}, u32[]{:S(2)}, u32[]{:S(2)}) async-start(f32[1,3,2048]{1,0,2:T(1,128)} %bitcast.50), calls=%async_computation.4 | async-start | bytes 2097152 | tf_op jit(solution)/shard_map/all_to_all | solution.py:236
  469.0 54.5 %copy-start.9 = (s32[2048]{0:T(1024)S(1)}, s32[2048]{0:T(1024)}, u32[]{:S(2)}) copy-start(s32[2048]{0:T(1024)} %broadcast_clamp_fusion.1) | copy-start | bytes 24580
  487.3 34.5 %all-to-all-start.5 = ((f32[1,3,2048]{1,0,2:T(1,128)}), f32[1,3,2048]{1,0,2:T(1,128)S(1)}, u32[]{:S(2)}, u32[]{:S(2)}) async-start(f32[1,3,2048]{1,0,2:T(1,128)} %bitcast.56), calls=%async_computation.5 | async-start | bytes 2097152 | tf_op jit(solution)/shard_map/all_to_all | solution.py:237
  536.5 11.9 %copy-start.8 = (f32[8,1,256]{2,1,0:T(1,128)S(1)}, f32[8,1,256]{2,1,0:T(1,128)}, u32[]{:S(2)}) copy-start(f32[8,1,256]{2,1,0:T(1,128)} %copy-done.7) | copy-start | bytes 24580
  536.6 11.9 %copy-start.13 = (f32[8,256]{1,0:T(8,128)S(1)}, f32[8,256]{1,0:T(8,128)}, u32[]{:S(2)}) copy-start(f32[8,256]{1,0:T(8,128)} %param.24) | copy-start | bytes 24580
  536.6 29.3 %copy-start.3 = (f32[8,8,1,256]{3,2,1,0:T(1,128)S(1)}, f32[8,8,1,256]{3,2,1,0:T(1,128)}, u32[]{:S(2)}) copy-start(f32[8,8,1,256]{3,2,1,0:T(1,128)} %param.21) | copy-start | bytes 196612
  536.6 36.0 %copy-start.2 = (f32[8,8,1,256]{3,2,1,0:T(1,128)S(1)}, f32[8,8,1,256]{3,2,1,0:T(1,128)}, u32[]{:S(2)}) copy-start(f32[8,8,1,256]{3,2,1,0:T(1,128)} %param.22) | copy-start | bytes 196612
  536.6 229.2 %copy-start.11 = (s32[2]{0:T(128)S(1)}, s32[2]{0:T(128)}, u32[]{:S(2)}) copy-start(s32[2]{0:T(128)} %constant.307.clone.1) | copy-start | bytes 28
  549.1 13.5 %all-to-all-start.7 = ((f32[1,8,256]{2,0,1:T(1,128)}), f32[1,8,256]{2,0,1:T(1,128)S(1)}, u32[]{:S(2)}, u32[]{:S(2)}) async-start(f32[1,8,256]{2,0,1:T(1,128)} %copy.82), calls=%async_computation.7 | async-start | bytes 16384 | tf_op jit(solution)/shard_map/all_to_all | solution.py:254
  562.6 9.9 %all-to-all-start.6 = ((f32[1,8,256]{2,0,1:T(1,128)}), f32[1,8,256]{2,0,1:T(1,128)S(1)}, u32[]{:S(2)}, u32[]{:S(2)}) async-start(f32[1,8,256]{2,0,1:T(1,128)} %copy.80), calls=%async_computation.6 | async-start | bytes 16384 | tf_op jit(solution)/shard_map/all_to_all | solution.py:247
  835.0 3.4 copy-start.1
  835.0 3.4 copy-start.4
where the time goes:
time: 849 us; the launch traced here: 839 us
  blocking collectives  438 us (52%)
  local copies, waits for them, and re-layouts  174 us (20%)
  starting transfers between devices  67.8 us (8%)
  matrix products  61.9 us (7%)
  other arithmetic  47.7 us (6%)
  waiting for transfers between devices  42 us (5%)
    psum x1, blocking collectives, body(): sum_re, sum_im = lax.psum((part_re, part_im), 'pw')  246 us
    psum x1, blocking collectives, body(): coef_re, coef_im = lax.psum((part_re, part_im), ('band', 'pw'))  97.3 us
    psum x1, blocking collectives, body(): gram_re, gram_im = lax.psum((gram_re, gram_im), ('band', 'pw'))  94.5 us
    all_to_all x1, waiting for transfers between devices, body(): lax.all_to_all(out_im, 'pw', split_axis=2, concat_axis=1, tiled=True)  25.4 us
    convert_element_type x1, other arithmetic, phase_table(): jnp.cos(angle).astype(jnp.bfloat16)  20.4 us
  transfers between devices with their start and end apart: 8, of which 4 were waited for; matrix products, arithmetic and copies ran while one was open for 14% of the time, Pallas kernels for 0%

commit v1 on v0

v1 whole, which is shorter than its diff:
```python
import math

import jax
import jax.numpy as jnp
import numpy as np
from jax import lax
from jax.experimental import pallas as pl
from jax.experimental.pallas import tpu as pltpu
from jax.sharding import PartitionSpec as P

f32 = jnp.float32
bf16 = jnp.bfloat16
exact_mode = lax.Precision.HIGHEST

COS_POLY = (0.9999999403953552, -4.934792995452881, 4.058411121368408, -1.331876516342163, 0.21968960762023926)
SIN_POLY = (3.1415927410125732, -5.167710304260254, 2.550077438354492, -0.598291277885437, 0.07765766233205795)


def dot(left, right, left_dim=1, right_dim=0, precision=None):
    return lax.dot_general(
        left,
        right,
        (((left_dim,), (right_dim,)), ((), ())),
        precision=precision,
        preferred_element_type=f32,
    )


def split(part):
    high = part.astype(bf16)
    return high, (part - high.astype(f32)).astype(bf16)


def dot3(left, right, left_dim=1, right_dim=0):
    lh, ll = left
    rh, rl = right
    return (
        dot(lh, rh, left_dim, right_dim)
        + dot(ll, rh, left_dim, right_dim)
        + dot(lh, rl, left_dim, right_dim)
    )


def transform_tables(grid, planes):
    cos = np.array([math.cos(2.0 * math.pi * t / grid) for t in range(grid)])
    sin = np.array([math.sin(2.0 * math.pi * t / grid) for t in range(grid)])
    ticks = np.arange(grid)
    turns = ticks[:, None] * ticks[None, :] % grid
    order = ticks.reshape(grid // planes, planes).T.reshape(-1)

    def pieces(table):
        table = table.astype(np.float32)
        high = table.astype(jnp.bfloat16)
        low = (table - high.astype(np.float32)).astype(jnp.bfloat16)
        return [high, low]

    flat = np.stack(pieces(cos[turns]) + pieces(sin[turns]))
    by_owner = np.stack(pieces(cos[turns[order]]) + pieces(sin[turns[order]]))
    return flat, by_owner


def stripes(part, count):
    rows = part.shape[0] // count
    return jnp.concatenate([part[i * rows : (i + 1) * rows] for i in range(count)], 1)


def unstripe(part, count):
    width = part.shape[1] // count
    return jnp.concatenate([part[:, i * width : (i + 1) * width] for i in range(count)], 0)


def kernel_call(kernel, outs, *args, flops=10**6, vmem=32):
    return pl.pallas_call(
        kernel,
        out_shape=outs,
        in_specs=[pl.BlockSpec(memory_space=pltpu.VMEM)] * len(args),
        out_specs=jax.tree.map(lambda _: pl.BlockSpec(memory_space=pltpu.VMEM), outs),
        compiler_params=pltpu.CompilerParams(vmem_limit_bytes=vmem * 2**20),
        cost_estimate=pl.CostEstimate(flops=flops, bytes_accessed=4 * 10**6, transcendentals=0),
    )(*args)


def shape(*dims, dtype=f32):
    return jax.ShapeDtypeStruct(dims, dtype)


def pack_kernel(re_ref, im_ref, basis_ref, send_ref):
    rows = re_ref.shape[0] // 2
    bands = send_ref.shape[0]

    def whole(ref):
        return jnp.concatenate(
            [ref[pl.ds(0, rows, stride=2), :], ref[pl.ds(1, rows, stride=2), :]], 1
        )

    basis = jnp.concatenate([whole(re_ref), whole(im_ref)], 0)
    basis_ref[...] = basis
    mixed = dot(basis, basis, 1, 1, exact_mode)
    over_re = mixed[:rows, :rows] + mixed[rows:, rows:]
    over_im = mixed[:rows, rows:] - mixed[rows:, :rows]
    line = lax.broadcasted_iota(jnp.int32, (rows, rows), 0)
    spot = lax.broadcasted_iota(jnp.int32, (rows, rows), 1)
    packed = stripes(jnp.where(line <= spot, over_re, over_im), 2)
    first = 2 * (rows - bands)
    for band in range(bands):
        send_ref[band, 0:2, :] = re_ref[first + 2 * band : first + 2 * band + 2, :]
        send_ref[band, 2:4, :] = im_ref[first + 2 * band : first + 2 * band + 2, :]
        send_ref[band, 4:8, :] = packed[4 * band : 4 * band + 4, :]


def phase_kernel(grid, columns, map_ref, place_ref, sites_ref, phase_ref):
    atoms = sites_ref.shape[0]
    groups, rows = map_ref.shape
    sites = sites_ref[...].astype(bf16)
    column_x = place_ref[:, 0:1].astype(f32)
    column_y = place_ref[:, 1:2].astype(f32)
    ticks = lax.broadcasted_iota(jnp.int32, (columns, rows), 0)
    for s in range(groups):
        cell = map_ref[s : s + 1, :]
        depth = lax.div(cell, columns).astype(f32)
        hot = ticks == lax.rem(cell, columns)
        x = jnp.sum(jnp.where(hot, column_x, 0.0), 0, keepdims=True)
        y = jnp.sum(jnp.where(hot, column_y, 0.0), 0, keepdims=True)
        place = jnp.concatenate([depth, x, y, jnp.zeros((5, rows), f32)], 0).astype(bf16)
        turns = dot(sites, place)
        turns = turns - grid * jnp.floor(turns * (1.0 / grid) + 0.5)
        u = turns * (1.0 / grid)
        w = u * u
        c = COS_POLY[4]
        for k in (3, 2, 1, 0):
            c = c * w + COS_POLY[k]
        h = SIN_POLY[4]
        for k in (3, 2, 1, 0):
            h = h * w + SIN_POLY[k]
        h = h * u
        twice = h + h
        phase_ref[0:atoms, s * rows : (s + 1) * rows] = (1.0 - twice * h).astype(bf16)
        phase_ref[atoms : 2 * atoms, s * rows : (s + 1) * rows] = (twice * c).astype(bf16)


def two_rows(ref, s, line):
    return jnp.concatenate([ref[s, line : line + 1, :], ref[s, line + 1 : line + 2, :]], 1)


def columns_kernel(columns, map_ref, form_ref, phase_ref, table_ref, got_ref, send_ref):
    groups, rows = map_ref.shape
    atoms = phase_ref.shape[0] // 2
    grid = table_ref.shape[1]
    planes = send_ref.shape[1]
    owners = send_ref.shape[0]
    channels = form_ref.shape[0]
    ticks = lax.broadcasted_iota(jnp.int32, (columns, rows), 0)
    deep = lax.broadcasted_iota(jnp.int32, (grid, rows), 0)
    total = jnp.zeros((4 * columns, grid), f32)
    first, second = [], []
    for s in range(groups):
        psi_re = two_rows(got_ref, s, 0)
        psi_im = two_rows(got_ref, s, 2)
        cell = map_ref[s : s + 1, :]
        depth_hot = (deep == lax.div(cell, columns)).astype(f32).astype(bf16)
        hot = ticks == lax.rem(cell, columns)
        spread = jnp.concatenate([jnp.where(hot, psi_re, 0.0), jnp.where(hot, psi_im, 0.0)], 0)
        total = total + dot(jnp.concatenate(split(spread), 0), depth_hot, 1, 1)
        form = form_ref[:, s, :]
        weighted_re = (form * psi_re).astype(bf16)
        weighted_im = (form * psi_im).astype(bf16)
        first.append(jnp.concatenate([weighted_re, weighted_im], 0))
        second.append(jnp.concatenate([-weighted_im, weighted_re], 0))
    column = split(total[: 2 * columns] + total[2 * columns :])
    by_cos = dot3((table_ref[0], table_ref[1]), column, 1, 1)
    by_sin = dot3((table_ref[2], table_ref[3]), column, 1, 1)
    deep_re = by_cos[:, :columns] - by_sin[:, columns:]
    deep_im = by_sin[:, :columns] + by_cos[:, columns:]
    products = dot(phase_ref[0:atoms, :], jnp.concatenate(first, 1), 1, 1) + dot(
        phase_ref[atoms : 2 * atoms, :], jnp.concatenate(second, 1), 1, 1
    )
    parts = [products[owners * k : owners * (k + 1)] for k in range(atoms // owners)]
    half = len(parts) // 2
    overlap = jnp.sum(got_ref[:, 4:8, :], 0).T
    own = jnp.concatenate(
        [overlap[:owners], overlap[owners:], jnp.zeros((owners, 2 * columns - 8), f32)], 1
    )
    extra = [
        jnp.concatenate(parts[:half], 1),
        jnp.concatenate(parts[half:], 1),
        own,
    ]
    for k in range(planes):
        lines = slice(owners * k, owners * (k + 1))
        send_ref[:, k, :] = jnp.concatenate([deep_re[lines], deep_im[lines], extra[k]], 1)


def planes_kernel(columns, place_ref, pot_ref, table_ref, got_ref, send_ref):
    planes, grid, _ = pot_ref.shape
    owners = got_ref.shape[0]
    steps, lanes = place_ref.shape[1:]
    packs = lanes // owners
    ticks = lax.broadcasted_iota(jnp.int32, (grid, lanes), 0)
    cos = (table_ref[0], table_ref[1])
    sin = (table_ref[2], table_ref[3])
    values = []
    for k in range(planes):
        turned = got_ref[:, k, :].T
        for part in range(2):
            high, low = split(stripes(turned[part * columns : (part + 1) * columns], packs))
            values.append((high.astype(f32), low.astype(f32)))
    field = jnp.zeros((2 * planes * grid, grid), f32)
    hots = []
    for q in range(steps):
        hot_x = ticks == place_ref[0, q : q + 1, :]
        hot_y = (ticks == place_ref[1, q : q + 1, :]).astype(f32).astype(bf16)
        hots.append((hot_x, hot_y))
        for piece in range(2):
            spread = jnp.concatenate(
                [jnp.where(hot_x, v[piece][q : q + 1, :], 0.0).astype(bf16) for v in values], 0
            )
            field = field + dot(spread, hot_y, 1, 1)

    def along_y(parts):
        pieces = split(jnp.concatenate(parts, 0))
        return dot3(pieces, cos), dot3(pieces, sin)

    parts = [field[i * grid : (i + 1) * grid] for i in range(2 * planes)]
    by_cos, by_sin = along_y(parts)
    back = []
    for k in range(planes):
        re = slice(2 * k * grid, (2 * k + 1) * grid)
        im = slice((2 * k + 1) * grid, (2 * k + 2) * grid)
        now_re = split(by_cos[re] - by_sin[im])
        now_im = split(by_sin[re] + by_cos[im])
        real = dot3(cos, now_re) - dot3(sin, now_im)
        imag = dot3(sin, now_re) + dot3(cos, now_im)
        scaled = pot_ref[k] * (1.0 / grid**3)
        real = split(real * scaled)
        imag = split(imag * scaled)
        back.append(dot3(cos, real) + dot3(sin, imag))
        back.append(dot3(cos, imag) - dot3(sin, real))
    by_cos, by_sin = along_y(back)
    final = []
    for k in range(planes):
        re = slice(2 * k * grid, (2 * k + 1) * grid)
        im = slice((2 * k + 1) * grid, (2 * k + 2) * grid)
        final.append(by_cos[re] + by_sin[im])
        final.append(by_cos[im] - by_sin[re])
    high, low = split(jnp.concatenate(final, 0))
    found = [[] for _ in final]
    for q in range(steps):
        hot_x, hot_y = hots[q]
        mixed = dot(high, hot_y) + dot(low, hot_y)
        for i in range(2 * planes):
            picked = jnp.where(hot_x, mixed[i * grid : (i + 1) * grid], 0.0)
            found[i].append(jnp.sum(picked, 0, keepdims=True))
    for k in range(planes):
        halves = [unstripe(jnp.concatenate(found[2 * k + i], 0), packs) for i in range(2)]
        turned = jnp.concatenate(halves, 0).T
        ride = jnp.sum(got_ref[:, k, 2 * columns :], 0, keepdims=True)
        send_ref[:, k, :] = jnp.concatenate(
            [turned, jnp.broadcast_to(ride, (owners, ride.shape[1]))], 1
        )


def image_kernel(
    columns, waves, map_ref, form_ref, kinetic_ref, strength_ref, phase_ref, table_ref, psi_ref, got_ref, send_ref
):
    groups, rows = map_ref.shape
    atoms = phase_ref.shape[0] // 2
    grid = table_ref.shape[1]
    owners, planes, _ = got_ref.shape
    channels = form_ref.shape[0]
    root = math.sqrt(waves)
    got = [got_ref[:, k, :] for k in range(planes)]
    ride = [g[:, 2 * columns :] for g in got]
    wide = 2 * channels
    per_row = 2 * columns // wide
    sums = jnp.concatenate(
        [r[:, wide * i : wide * (i + 1)] for r in ride[:2] for i in range(per_row)], 0
    ).T
    factor = jnp.concatenate([strength_ref[...], strength_ref[...]], 0)
    scaled = factor * (sums / root) / root
    scaled_re = scaled[:channels].astype(bf16)
    scaled_im = scaled[channels:].astype(bf16)
    mixed = dot(jnp.concatenate([scaled_re, scaled_im], 0), phase_ref[0:atoms, :]) + dot(
        jnp.concatenate([scaled_im, -scaled_re], 0), phase_ref[atoms : 2 * atoms, :]
    )
    deep = split(jnp.concatenate([g[:, : 2 * columns] for g in got], 0).T)
    by_cos = dot3(deep, (table_ref[0], table_ref[1]))
    by_sin = dot3(deep, (table_ref[2], table_ref[3]))
    out_re = by_cos[:columns] + by_sin[columns:]
    out_im = by_cos[columns:] - by_sin[:columns]
    out = jnp.concatenate(split(jnp.concatenate([out_re, out_im], 0)), 0)
    ticks = lax.broadcasted_iota(jnp.int32, (columns, rows), 0)
    depths = lax.broadcasted_iota(jnp.int32, (grid, rows), 0)
    overlap = jnp.concatenate([ride[2][:, 0:4].T, ride[2][:, 4:8].T], 1)
    for s in range(groups):
        cell = map_ref[s : s + 1, :]
        depth_hot = (depths == lax.div(cell, columns)).astype(f32).astype(bf16)
        hot = ticks == lax.rem(cell, columns)
        found = dot(out, depth_hot)
        found = found[: 2 * columns] + found[2 * columns :]
        local_re = jnp.sum(jnp.where(hot, found[:columns], 0.0), 0, keepdims=True)
        local_im = jnp.sum(jnp.where(hot, found[columns:], 0.0), 0, keepdims=True)
        form = form_ref[:, s, :]
        lanes = slice(s * rows, (s + 1) * rows)
        near_re = jnp.sum(form * mixed[:channels, lanes], 0, keepdims=True)
        near_im = jnp.sum(form * mixed[channels:, lanes], 0, keepdims=True)
        kinetic = kinetic_ref[s : s + 1, :]
        image_re = kinetic * two_rows(psi_ref, s, 0) + local_re + near_re
        image_im = kinetic * two_rows(psi_ref, s, 2) + local_im + near_im
        send_ref[s, 0:1, :] = image_re[:, :128]
        send_ref[s, 1:2, :] = image_re[:, 128:]
        send_ref[s, 2:3, :] = image_im[:, :128]
        send_ref[s, 3:4, :] = image_im[:, 128:]
        send_ref[s, 4:8, :] = overlap


def products_kernel(waves, basis_ref, got_ref, image_ref, send_ref):
    bands = got_ref.shape[0]
    half = basis_ref.shape[0] // 2
    owners = send_ref.shape[0]
    image_re = jnp.concatenate([got_ref[:, 0, :], got_ref[:, 1, :]], 1)
    image_im = jnp.concatenate([got_ref[:, 2, :], got_ref[:, 3, :]], 1)
    image = jnp.concatenate([image_re, image_im], 0)
    image_ref[...] = image
    mixed = dot(image, basis_ref[...], 1, 1, exact_mode) * (1.0 / waves)
    coef_re = mixed[:bands, :half] + mixed[bands:, half:]
    coef_im = mixed[bands:, :half] - mixed[:bands, half:]
    coef = jnp.concatenate([coef_re, coef_im], 1)
    own = dot(image, image, 1, 1, exact_mode) * (1.0 / waves)
    own_re = own[:bands, :bands] + own[bands:, bands:]
    own_im = own[:bands, bands:] - own[bands:, :bands]
    line = lax.broadcasted_iota(jnp.int32, (bands, bands), 0)
    spot = lax.broadcasted_iota(jnp.int32, (bands, bands), 1)
    packed = jnp.where(line <= spot, own_re, own_im)
    row = jnp.concatenate(
        [stripes(coef, bands), stripes(packed, bands), jnp.zeros((1, 128 - bands * bands), f32)], 1
    )
    send_ref[:, 0, :] = jnp.broadcast_to(row, (owners, row.shape[1]))


def overlap_kernel(waves, got_ref, over_ref):
    size = over_ref.shape[0] // 2
    packed = jnp.concatenate([got_ref[d, 4:8, :] for d in range(got_ref.shape[0])], 0)
    packed = unstripe(packed, 2) * (1.0 / waves)
    line = lax.broadcasted_iota(jnp.int32, (size, size), 0)
    spot = lax.broadcasted_iota(jnp.int32, (size, size), 1)
    turned = packed.T
    over_re = jnp.where(line <= spot, packed, turned)
    over_im = jnp.where(line < spot, -turned, jnp.where(line > spot, packed, 0.0))
    over_ref[...] = jnp.concatenate(
        [jnp.concatenate([over_re, -over_im], 1), jnp.concatenate([over_im, over_re], 1)], 0
    )


def gather_kernel(got_ref, send_ref):
    row = jnp.sum(got_ref[:, 0, :], 0, keepdims=True)
    send_ref[:, 0, :] = jnp.broadcast_to(row, (send_ref.shape[0], row.shape[1]))


def finish_kernel(
    basis_ref, image_ref, over_ref, got_ref, next_re_ref, next_im_ref, coef_re_ref, coef_im_ref, chol_re_ref, chol_im_ref
):
    bands = image_ref.shape[0] // 2
    half = basis_ref.shape[0] // 2
    row = jnp.sum(got_ref[:, 0, :], 0, keepdims=True)
    size = bands * 2 * half
    coef = unstripe(row[:, :size], bands)
    packed = unstripe(row[:, size : size + bands * bands], bands)
    coef_re = coef[:, :half]
    coef_im = coef[:, half:]
    coef_re_ref[...] = coef_re.T
    coef_im_ref[...] = coef_im.T
    line = lax.broadcasted_iota(jnp.int32, (bands, bands), 0)
    spot = lax.broadcasted_iota(jnp.int32, (bands, bands), 1)
    turned = packed.T
    own_re = jnp.where(line <= spot, packed, turned)
    own_im = jnp.where(line < spot, -turned, jnp.where(line > spot, packed, 0.0))
    left = dot(coef, over_ref[...], 1, 0, exact_mode) - 2.0 * coef
    stacked = jnp.concatenate([coef, jnp.concatenate([-coef_im, coef_re], 1)], 0)
    mixed = dot(stacked, left, 1, 1, exact_mode)
    gram_re = own_re + mixed[:bands]
    gram_im = own_im + mixed[bands:]
    eye = jnp.where(line == spot, 1.0, 0.0)
    work_re = jnp.concatenate([gram_re, eye], 1)
    work_im = jnp.concatenate([gram_im, jnp.zeros_like(eye)], 1)
    rows_re, rows_im = [], []
    for k in range(bands):
        pivot = lax.rsqrt(work_re[k : k + 1, k : k + 1])
        lead_re = work_re[k : k + 1, :] * pivot
        lead_im = work_im[k : k + 1, :] * pivot
        rows_re.append(lead_re)
        rows_im.append(lead_im)
        if k + 1 < bands:
            column_re = work_re[:, k : k + 1] * pivot
            column_im = work_im[:, k : k + 1] * pivot
            work_re, work_im = (
                work_re - (column_re * lead_re - column_im * lead_im),
                work_im - (column_re * lead_im + column_im * lead_re),
            )
    all_re = jnp.concatenate(rows_re, 0)
    all_im = jnp.concatenate(rows_im, 0)
    chol_re_ref[...] = jnp.where(line <= spot, all_re[:, :bands], 0.0)
    chol_im_ref[...] = jnp.where(line < spot, all_im[:, :bands], 0.0)
    inv_re = all_re[:, bands:]
    inv_im = all_im[:, bands:]
    basis_re = basis_ref[0:half, :]
    basis_im = basis_ref[half : 2 * half, :]
    span_re = dot(coef, jnp.concatenate([basis_re, -basis_im], 0), 1, 0, exact_mode)
    span_im = dot(coef, jnp.concatenate([basis_im, basis_re], 0), 1, 0, exact_mode)
    rest_re = image_ref[0:bands, :] - span_re
    rest_im = image_ref[bands : 2 * bands, :] - span_im
    next_re = dot(inv_re, rest_re, 1, 0, exact_mode) + dot(inv_im, rest_im, 1, 0, exact_mode)
    next_im = dot(inv_re, rest_im, 1, 0, exact_mode) - dot(inv_im, rest_re, 1, 0, exact_mode)
    for ref, value in ((next_re_ref, next_re), (next_im_ref, next_im)):
        ref[pl.ds(0, bands, stride=2), :] = value[:, :128]
        ref[pl.ds(1, bands, stride=2), :] = value[:, 128:]


def body(
    basis_re,
    basis_im,
    potential,
    kinetic,
    form_factors,
    channel_strength,
    sphere_map,
    column_map,
    atom_sites,
):
    blocks, slab, _, row_count = basis_re.shape
    band_count = lax.axis_size("band")
    owners = lax.axis_size("pw")
    planes, grid, _ = potential.shape
    columns = column_map.shape[0] // owners
    waves = band_count * owners * row_count
    atoms = atom_sites.shape[1]
    rows = blocks * slab
    flat_table, owner_table = transform_tables(grid, planes)
    flat_table = jnp.asarray(flat_table)
    owner_table = jnp.asarray(owner_table)

    def exchange(part, axis):
        return lax.all_to_all(part, axis, split_axis=0, concat_axis=0, tiled=True)

    basis, send = kernel_call(
        pack_kernel,
        (shape(2 * rows, row_count), shape(slab, 8, 128)),
        basis_re.reshape(-1, 128),
        basis_im.reshape(-1, 128),
    )
    psi = exchange(send, "band")

    x_index = column_map // grid
    y_index = column_map % grid
    both = jnp.stack([x_index, y_index])
    mine = lax.dynamic_slice_in_dim(both, lax.axis_index("pw") * columns, columns, 1).T
    spread = both.reshape(2, owners, columns // 8, 8).transpose(0, 3, 2, 1).reshape(2, 8, -1)
    sites = jnp.pad(atom_sites, ((0, 5), (0, 0))).T.astype(f32)
    phase = kernel_call(
        lambda *refs: phase_kernel(grid, columns, *refs),
        shape(2 * atoms, band_count * row_count, dtype=bf16),
        sphere_map,
        mine,
        sites,
        flops=10**7,
    )
    send = kernel_call(
        lambda *refs: columns_kernel(columns, *refs),
        shape(owners, planes, 128),
        sphere_map,
        form_factors,
        phase,
        owner_table,
        psi,
    )
    got = exchange(send, "pw")
    send = kernel_call(
        lambda *refs: planes_kernel(columns, *refs),
        shape(owners, planes, 128),
        spread,
        potential,
        flat_table,
        got,
        vmem=48,
    )
    got = exchange(send, "pw")
    send = kernel_call(
        lambda *refs: image_kernel(columns, waves, *refs),
        shape(band_count, 8, 128),
        sphere_map,
        form_factors,
        kinetic,
        channel_strength[:, None],
        phase,
        owner_table,
        psi,
        got,
    )
    got = exchange(send, "band")
    image, send = kernel_call(
        lambda *refs: products_kernel(waves, *refs),
        (shape(2 * slab, row_count), shape(owners, 1, 9 * 128)),
        basis,
        got,
    )
    over = kernel_call(
        lambda *refs: overlap_kernel(waves, *refs), shape(2 * rows, 2 * rows), got
    )
    got = exchange(send, "pw")
    send = kernel_call(gather_kernel, shape(band_count, 1, 9 * 128), got)
    got = exchange(send, "band")
    next_re, next_im, coef_re, coef_im, chol_re, chol_im = kernel_call(
        finish_kernel,
        (
            shape(2 * slab, 128),
            shape(2 * slab, 128),
            shape(rows, slab),
            shape(rows, slab),
            shape(slab, slab),
            shape(slab, slab),
        ),
        basis,
        image,
        over,
        got,
    )
    return (
        next_re.reshape(slab, 1, row_count),
        next_im.reshape(slab, 1, row_count),
        coef_re.reshape(blocks, slab, slab),
        coef_im.reshape(blocks, slab, slab),
        chol_re,
        chol_im,
    )


def solution(mesh):
    return jax.shard_map(
        body,
        mesh=mesh,
        in_specs=(
            P(None, None, "band", "pw"),
            P(None, None, "band", "pw"),
            P("pw", None, None),
            P(None, "pw"),
            P(None, None, "pw"),
            P(),
            P(None, "pw"),
            P(),
            P(),
        ),
        out_specs=(P(None, "band", "pw"), P(None, "band", "pw"), P(), P(), P(), P()),
        check_vma=False,
    )
```

time: 849 us -> 132 us (0.16); the launches traced: 839 us -> 132 us
  blocking collectives: 438 us -> 32.5 us
  local copies, waits for them, and re-layouts: 174 us -> 10.4 us
  matrix products: 61.9 us -> 0 us
  other arithmetic: 47.7 us -> 0.82 us
  starting transfers between devices: 67.8 us -> 29.7 us
  Pallas kernels: 0 us -> 29.1 us
  waiting for transfers between devices: 42 us -> 28.3 us
    psum x3 -> x0, blocking collectives: 438 us -> none  [the longest x1 246 us: body(): sum_re, sum_im = lax.psum((part_re, part_im), 'pw')]
    gather x7 -> x0, local copies, waits for them, and re-layouts: 63.3 us -> none  [the longest x1 14 us: body(): joint[:, :, :, grid:].reshape(count, planes, grid * grid)[:, :, column_map]]
    dot_general x94 -> x0, matrix products: 61.9 us -> none  [the longest x8 11.7 us: apply(): return jnp.einsum('pz,bzc->bpc', table, part, precision=exact_mode)]
    scatter x36 -> x0, local copies, waits for them, and re-layouts: 44.1 us -> none  [the longest x1 13.5 us: body(): empty.at[:, :, column_map].set(part_im).reshape(count, planes, grid, grid)]
    reshape x6 -> x1, local copies, waits for them, and re-layouts: 42.9 us -> 0.09 us  [body(): both.reshape(2, owners, columns // 8, 8).transpose(0, 3, 2, 1)]
    all_to_all x8 -> x4, starting transfers between devices: 67.8 us -> 29.7 us  [exchange(): return lax.all_to_all(part, axis, split_axis=0, concat_axis=0, tiled=True)]
    all_to_all x0 -> x2, blocking collectives: none -> 32.5 us  [exchange(): return lax.all_to_all(part, axis, split_axis=0, concat_axis=0, tiled=True)]
    pallas_call x0 -> x9, Pallas kernels: none -> 29.1 us  [kernel_call(): pl.pallas_call(kernel, out_shape=outs, in_specs=[pl.BlockSpec(memory_spac...]
  transfers between devices with their start and end apart: 8 -> 4, of which waited for: 4 -> 3; matrix products, arithmetic and copies ran while one was open for 14% -> 2% of each run, Pallas kernels for 0% -> 3%
where the time goes in v1:
time: 132 us
  blocking collectives  32.5 us (25%)
  starting transfers between devices  29.7 us (22%)
  Pallas kernels  29.1 us (22%)
  waiting for transfers between devices  28.3 us (21%)
  local copies, waits for them, and re-layouts  10.4 us (8%)
    all_to_all x2, blocking collectives, exchange(): return lax.all_to_all(part, axis, split_axis=0, concat_axis=0, tiled=True)  32.5 us
    all_to_all x4, starting transfers between devices, exchange(): return lax.all_to_all(part, axis, split_axis=0, concat_axis=0, tiled=True)  29.7 us
    pallas_call x9, Pallas kernels, kernel_call(): pl.pallas_call(kernel, out_shape=outs, in_specs=[pl.BlockSpec(memory_spac...  29.1 us
    all_to_all x4, waiting for transfers between devices, exchange(): return lax.all_to_all(part, axis, split_axis=0, concat_axis=0, tiled=True)  28.3 us
    unnamed x28, local copies, waits for them, and re-layouts  9.69 us
  transfers between devices with their start and end apart: 4, of which 3 were waited for; matrix products, arithmetic and copies ran while one was open for 2% of the time, Pallas kernels for 3%

profile of v1, /device:TPU:1, one launch (start us, length us, event | category | flops | bytes accessed | tf_op | source)
XLA Modules:
  0.0 131.7 jit_solution(6280292580090074878)
XLA Ops:
  0.7 0.9 copy-done.9
  1.6 0.8 copy-done.10
  2.4 1.1 shard_map.154
  3.5 10.9 %all-to-all-start = ((f32[8,8,128]{2,1,0:T(8,128)}), f32[8,8,128]{2,1,0:T(8,128)S(1)}, u32[]{:S(2)}, u32[]{:S(2)}) async-start(f32[8,8,128]{2,1,0:T(8,128)} %get-tuple-element.17), calls=%async_computation | async-start | bytes 65536 | tf_op jit(solution)/shard_map/all_to_all | solution.py:442
  14.4 0.7 add_select_fusion
  15.1 0.8 copy.29
  16.0 0.1 copy.36
  16.1 0.7 copy-done.7
  16.8 4.3 %shard_map.155.refs_2_.refs_4_ = bf16[1024,2048]{1,0:T(8,128)(2,1)S(1)} custom-call(s32[8,256]{1,0:T(8,128)S(1)} %copy-done.7, s32[32,2]{1,0:T(8,128)S(1)} %bitcast.14, f32[512,8]{1,0:T(8,128)S(1)} %convert_bitcast_fusion.refs_2_), custom_call_target="tpu_custom_call" | custom-call | flops 10000000 | bytes 4000000 | tf_op jit(solution)/shard_map/pallas_call | solution.py:73
  21.1 1.9 %copy-done = bf16[1024,2048]{1,0:T(8,128)(2,1)} copy-done((bf16[1024,2048]{1,0:T(8,128)(2,1)}, bf16[1024,2048]{1,0:T(8,128)(2,1)S(1)}, u32[]{:S(2)}) %copy-start) | copy-done | bytes 4194328
  23.1 2.2 %copy-done.1 = bf16[1024,2048]{1,0:T(8,128)(2,1)S(1)} copy-done((bf16[1024,2048]{1,0:T(8,128)(2,1)S(1)}, bf16[1024,2048]{1,0:T(8,128)(2,1)}, u32[]{:S(2)}) %copy-start.1) | copy-done | bytes 4194328
  25.3 3.0 %shard_map.156 = f32[64,3,128]{2,1,0:T(4,128)} custom-call(s32[8,256]{1,0:T(8,128)S(1)} %copy-done.8, f32[8,8,256]{2,1,0:T(8,128)S(1)} %copy-done.6, bf16[1024,2048]{1,0:T(8,128)(2,1)S(1)} %copy-done.1, bf16[4,192,192]{2,1,0:T(8,128)(2,1)S(1)} %copy-done.3, f32[8,8,128]{2,1,0:T(8,128)S(1)} %all-to-all-done.refs_4_.refs_6_), custom_call_target="tpu_custom_call" | custom-call | flops 1000000 | bytes 4000000 | tf_op jit(solution)/shard_map/pallas_call | solution.py:73
  28.2 11.1 %all-to-all-start.1 = ((f32[64,3,128]{2,1,0:T(4,128)}), f32[64,3,128]{2,1,0:T(4,128)S(1)}, u32[]{:S(2)}, u32[]{:S(2)}) async-start(f32[64,3,128]{2,1,0:T(4,128)} %shard_map.156), calls=%async_computation.1 | async-start | bytes 262144 | tf_op jit(solution)/shard_map/all_to_all | solution.py:442
  39.3 0.2 stack.18
  39.5 0.2 stack.19
  39.8 0.1 copy.31
  39.9 0.1 reshape.40.refs_0_
  40.0 10.4 %all-to-all-done.1.refs_3_ = f32[64,3,128]{2,1,0:T(4,128)S(1)} async-done(((f32[64,3,128]{2,1,0:T(4,128)}), f32[64,3,128]{2,1,0:T(4,128)S(1)}, u32[]{:S(2)}, u32[]{:S(2)}) %all-to-all-start.1) | async-done | bytes 98336 | tf_op jit(solution)/shard_map/all_to_all | solution.py:442
  50.4 16.1 %shard_map.157 = f32[64,3,128]{2,1,0:T(4,128)} custom-call(s32[2,8,256]{2,1,0:T(8,128)S(1)} %reshape.40.refs_0_, f32[3,192,192]{2,1,0:T(8,128)S(1)} %copy-done.4, bf16[4,192,192]{2,1,0:T(8,128)(2,1)S(1)} %copy-done.5, f32[64,3,128]{2,1,0:T(4,128)S(1)} %all-to-all-done.1.refs_3_), custom_call_target="tpu_custom_call" | custom-call | flops 1000000 | bytes 4000000 | tf_op jit(solution)/shard_map/pallas_call | solution.py:73
  66.5 4.4 %all-to-all-start.2 = ((f32[64,3,128]{2,1,0:T(4,128)}), f32[64,3,128]{2,1,0:T(4,128)S(1)}, u32[]{:S(2)}, u32[]{:S(2)}) async-start(f32[64,3,128]{2,1,0:T(4,128)} %shard_map.157), calls=%async_computation.2 | async-start | bytes 262144 | tf_op jit(solution)/shard_map/all_to_all | solution.py:442
  71.0 0.1 copy.33.refs_3_
  71.0 11.2 %all-to-all-done.2.refs_7_ = f32[64,3,128]{2,1,0:T(4,128)S(1)} async-done(((f32[64,3,128]{2,1,0:T(4,128)}), f32[64,3,128]{2,1,0:T(4,128)S(1)}, u32[]{:S(2)}, u32[]{:S(2)}) %all-to-all-start.2) | async-done | bytes 98336 | tf_op jit(solution)/shard_map/all_to_all | solution.py:442
  82.3 2.2 %copy-done.2 = bf16[1024,2048]{1,0:T(8,128)(2,1)S(1)} copy-done((bf16[1024,2048]{1,0:T(8,128)(2,1)S(1)}, bf16[1024,2048]{1,0:T(8,128)(2,1)}, u32[]{:S(2)}) %copy-start.2) | copy-done | bytes 4194328
  84.5 1.4 %shard_map.158 = f32[8,8,128]{2,1,0:T(8,128)S(1)} custom-call(s32[8,256]{1,0:T(8,128)S(1)} %copy-done.8, f32[8,8,256]{2,1,0:T(8,128)S(1)} %copy-done.6, f32[8,256]{1,0:T(8,128)S(1)} %copy-done.11, f32[8,1]{1,0:T(8,128)S(1)} %copy.33.refs_3_, bf16[1024,2048]{1,0:T(8,128)(2,1)S(1)} %copy-done.2, bf16[4,192,192]{2,1,0:T(8,128)(2,1)S(1)} %copy-done.3, ...), custom_call_target="tpu_custom_call" | custom-call | flops 1000000 | bytes 4000000 | tf_op jit(solution)/shard_map/pallas_call | solution.py:73
  85.9 13.7 %all_to_all.30.refs_1_.refs_0_ = f32[8,8,128]{2,1,0:T(8,128)S(1)} all-to-all(f32[8,8,128]{2,1,0:T(8,128)S(1)} %shard_map.158), channel_id=1, replica_groups=mesh['band'=8,'pw'=64] {'band'}, dimensions={0} | all-to-all | bytes 65536 | tf_op jit(solution)/shard_map/all_to_all | solution.py:442
  99.6 0.5 shard_map.159
  100.1 18.8 %all_to_all.31.got_ref = f32[64,1,1152]{2,1,0:T(1,128)S(1)} all-to-all(f32[64,1,1152]{2,1,0:T(1,128)S(1)} %get-tuple-element.19), channel_id=1, replica_groups=mesh['band'=8,'pw'=64] {'pw'}, dimensions={0} | all-to-all | bytes 589824 | tf_op jit(solution)/shard_map/all_to_all | solution.py:442
  118.9 0.7 shard_map.161
  119.6 3.3 %all-to-all-start.5 = ((f32[8,1,1152]{2,1,0:T(1,128)}), f32[8,1,1152]{2,1,0:T(1,128)S(1)}, u32[]{:S(2)}, u32[]{:S(2)}) async-start(f32[8,1,1152]{2,1,0:T(1,128)} %shard_map.161), calls=%async_computation.5 | async-start | bytes 73728 | tf_op jit(solution)/shard_map/all_to_all | solution.py:442
  123.0 0.2 shard_map.160.over_ref
  123.2 6.6 %all-to-all-done.5.got_ref = f32[8,1,1152]{2,1,0:T(1,128)S(1)} async-done(((f32[8,1,1152]{2,1,0:T(1,128)}), f32[8,1,1152]{2,1,0:T(1,128)S(1)}, u32[]{:S(2)}, u32[]{:S(2)}) %all-to-all-start.5) | async-done | bytes 36896 | tf_op jit(solution)/shard_map/all_to_all | solution.py:442
  129.8 1.9 %shard_map.162 = (f32[16,128]{1,0:T(8,128)}, f32[16,128]{1,0:T(8,128)}, f32[64,8]{1,0:T(8,128)}, f32[64,8]{1,0:T(8,128)}, f32[8,8]{1,0:T(8,128)}, /*index=5*/f32[8,8]{1,0:T(8,128)}) custom-call(f32[128,256]{1,0:T(8,128)S(1)} %get-tuple-element.16.refs_0_.basis_ref, f32[16,256]{1,0:T(8,128)S(1)} %get-tuple-element.18.image_ref, ...), custom_call_target="tpu_custom_call" | custom-call | flops 1000000 | bytes 4000000 | tf_op jit(solution)/shard_map/pallas_call | solution.py:73
  (26 shorter events, 0.3 us)
Async XLA Ops:
  0.6 22.4 %copy-start.3 = (bf16[4,192,192]{2,1,0:T(8,128)(2,1)S(1)}, bf16[4,192,192]{2,1,0:T(8,128)(2,1)}, u32[]{:S(2)}) copy-start(bf16[4,192,192]{2,1,0:T(8,128)(2,1)} %constant.34.clone.refs_3_.refs_5_) | copy-start | bytes 884740
  0.6 22.4 %copy-start.8 = (s32[8,256]{1,0:T(8,128)S(1)}, s32[8,256]{1,0:T(8,128)}, u32[]{:S(2)}) copy-start(s32[8,256]{1,0:T(8,128)} %refs_0_.5) | copy-start | bytes 24580
  0.7 22.4 %copy-start.6 = (f32[8,8,256]{2,1,0:T(8,128)S(1)}, f32[8,8,256]{2,1,0:T(8,128)}, u32[]{:S(2)}) copy-start(f32[8,8,256]{2,1,0:T(8,128)} %refs_1_.5) | copy-start | bytes 196612
  0.7 0.9 copy-start.9
  1.6 0.8 copy-start.10
  3.5 19.6 %all-to-all-start = ((f32[8,8,128]{2,1,0:T(8,128)}), f32[8,8,128]{2,1,0:T(8,128)S(1)}, u32[]{:S(2)}, u32[]{:S(2)}) async-start(f32[8,8,128]{2,1,0:T(8,128)} %get-tuple-element.17), calls=%async_computation | async-start | bytes 65536 | tf_op jit(solution)/shard_map/all_to_all | solution.py:442
  16.1 0.7 copy-start.7
  16.8 33.6 %copy-start.4 = (f32[3,192,192]{2,1,0:T(8,128)S(1)}, f32[3,192,192]{2,1,0:T(8,128)}, u32[]{:S(2)}) copy-start(f32[3,192,192]{2,1,0:T(8,128)} %refs_1_.4) | copy-start | bytes 1327108
  16.8 33.6 %copy-start.5 = (bf16[4,192,192]{2,1,0:T(8,128)(2,1)S(1)}, bf16[4,192,192]{2,1,0:T(8,128)(2,1)}, u32[]{:S(2)}) copy-start(bf16[4,192,192]{2,1,0:T(8,128)(2,1)} %constant.33.clone.refs_2_) | copy-start | bytes 884740
  21.1 1.9 %copy-start = (bf16[1024,2048]{1,0:T(8,128)(2,1)}, bf16[1024,2048]{1,0:T(8,128)(2,1)S(1)}, u32[]{:S(2)}) copy-start(bf16[1024,2048]{1,0:T(8,128)(2,1)S(1)} %shard_map.155.refs_2_.refs_4_) | copy-start | bytes 12582916
  23.1 2.2 %copy-start.1 = (bf16[1024,2048]{1,0:T(8,128)(2,1)S(1)}, bf16[1024,2048]{1,0:T(8,128)(2,1)}, u32[]{:S(2)}) copy-start(bf16[1024,2048]{1,0:T(8,128)(2,1)} %copy-done) | copy-start | bytes 12582916
  25.3 45.7 %copy-start.12 = (f32[8]{0:T(128)S(1)}, f32[8]{0:T(128)}, u32[]{:S(2)}) copy-start(f32[8]{0:T(128)} %param.16) | copy-start | bytes 100
  25.3 57.0 %copy-start.11 = (f32[8,256]{1,0:T(8,128)S(1)}, f32[8,256]{1,0:T(8,128)}, u32[]{:S(2)}) copy-start(f32[8,256]{1,0:T(8,128)} %refs_2_.2) | copy-start | bytes 24580
  28.2 22.2 %all-to-all-start.1 = ((f32[64,3,128]{2,1,0:T(4,128)}), f32[64,3,128]{2,1,0:T(4,128)S(1)}, u32[]{:S(2)}, u32[]{:S(2)}) async-start(f32[64,3,128]{2,1,0:T(4,128)} %shard_map.156), calls=%async_computation.1 | async-start | bytes 262144 | tf_op jit(solution)/shard_map/all_to_all | solution.py:442
  66.5 15.8 %all-to-all-start.2 = ((f32[64,3,128]{2,1,0:T(4,128)}), f32[64,3,128]{2,1,0:T(4,128)S(1)}, u32[]{:S(2)}, u32[]{:S(2)}) async-start(f32[64,3,128]{2,1,0:T(4,128)} %shard_map.157), calls=%async_computation.2 | async-start | bytes 262144 | tf_op jit(solution)/shard_map/all_to_all | solution.py:442
  82.3 2.2 %copy-start.2 = (bf16[1024,2048]{1,0:T(8,128)(2,1)S(1)}, bf16[1024,2048]{1,0:T(8,128)(2,1)}, u32[]{:S(2)}) copy-start(bf16[1024,2048]{1,0:T(8,128)(2,1)} %copy-done) | copy-start | bytes 12582916
  119.6 10.2 %all-to-all-start.5 = ((f32[8,1,1152]{2,1,0:T(1,128)}), f32[8,1,1152]{2,1,0:T(1,128)S(1)}, u32[]{:S(2)}, u32[]{:S(2)}) async-start(f32[8,1,1152]{2,1,0:T(1,128)} %shard_map.161), calls=%async_computation.5 | async-start | bytes 73728 | tf_op jit(solution)/shard_map/all_to_all | solution.py:442

commit v2 on v1

--- a/solution.py
+++ b/solution.py
@@ -31,6 +31,13 @@
     return high, (part - high.astype(f32)).astype(bf16)
 
 
+def split3(part):
+    high = part.astype(bf16)
+    rest = part - high.astype(f32)
+    middle = rest.astype(bf16)
+    return [high, middle, (rest - middle.astype(f32)).astype(bf16)]
+
+
 def dot3(left, right, left_dim=1, right_dim=0):
     lh, ll = left
     rh, rl = right
@@ -41,22 +48,34 @@
     )
 
 
-def transform_tables(grid, planes):
+def pieces(table):
+    table = table.astype(np.float32)
+    high = table.astype(jnp.bfloat16)
+    return [high, (table - high.astype(np.float32)).astype(jnp.bfloat16)]
+
+
+def transform_tables(grid, planes, half_x, half_y):
     cos = np.array([math.cos(2.0 * math.pi * t / grid) for t in range(grid)])
     sin = np.array([math.sin(2.0 * math.pi * t / grid) for t in range(grid)])
     ticks = np.arange(grid)
     turns = ticks[:, None] * ticks[None, :] % grid
     order = ticks.reshape(grid // planes, planes).T.reshape(-1)
-
-    def pieces(table):
-        table = table.astype(np.float32)
-        high = table.astype(jnp.bfloat16)
-        low = (table - high.astype(np.float32)).astype(jnp.bfloat16)
-        return [high, low]
-
-    flat = np.stack(pieces(cos[turns]) + pieces(sin[turns]))
     by_owner = np.stack(pieces(cos[turns[order]]) + pieces(sin[turns[order]]))
-    return flat, by_owner
+    top = grid // 2 + 1
+
+    def folded(half):
+        table = np.zeros((2 * half, 2 * half))
+        table[:top, :top] = cos[turns[:top, :top]]
+        table[half + 1 : half + top - 1, half + 1 : half + top - 1] = sin[
+            turns[1 : top - 1, 1 : top - 1]
+        ]
+        return pieces(table)
+
+    high, low = folded(half_x)
+    table_x = np.concatenate([high, low, high], 1)
+    high, low = folded(half_y)
+    table_y = np.concatenate([high, high, low], 0)
+    return by_owner, table_x, table_y
 
 
 def stripes(part, count):
@@ -69,22 +88,77 @@
     return jnp.concatenate([part[:, i * width : (i + 1) * width] for i in range(count)], 0)
 
 
-def kernel_call(kernel, outs, *args, flops=10**6, vmem=32):
-    return pl.pallas_call(
+def kernel_call(kernel, outs, *args, flops=10**6, vmem=8, scratch=(), far=(), far_out=(), grid=()):
+    single = not isinstance(outs, tuple)
+    outs = (outs,) if single else outs
+    place = (pl.BlockSpec(memory_space=pltpu.VMEM), pl.BlockSpec(memory_space=pltpu.HBM))
+    out = pl.pallas_call(
         kernel,
         out_shape=outs,
-        in_specs=[pl.BlockSpec(memory_space=pltpu.VMEM)] * len(args),
-        out_specs=jax.tree.map(lambda _: pl.BlockSpec(memory_space=pltpu.VMEM), outs),
+        in_specs=[place[i in far] for i in range(len(args))],
+        scratch_shapes=scratch,
+        grid=grid,
+        out_specs=tuple(place[i in far_out] for i in range(len(outs))),
         compiler_params=pltpu.CompilerParams(vmem_limit_bytes=vmem * 2**20),
         cost_estimate=pl.CostEstimate(flops=flops, bytes_accessed=4 * 10**6, transcendentals=0),
     )(*args)
+    return out[0] if single else out
 
 
 def shape(*dims, dtype=f32):
     return jax.ShapeDtypeStruct(dims, dtype)
 
 
-def pack_kernel(re_ref, im_ref, basis_ref, send_ref):
+def pack_kernel(
+    far_re_ref,
+    far_im_ref,
+    far_map_ref,
+    far_place_ref,
+    far_sites_ref,
+    basis_ref,
+    send_ref,
+    small_ref,
+    re_ref,
+    im_ref,
+    map_ref,
+    place_ref,
+    sites_ref,
+    sems,
+    small_sems,
+):
+    count = sems.shape[1]
+    small = [
+        pltpu.make_async_copy(far, near, small_sems.at[i])
+        for i, (far, near) in enumerate(
+            ((far_map_ref, map_ref), (far_place_ref, place_ref), (far_sites_ref, sites_ref))
+        )
+    ]
+    size = re_ref.shape[0] // count
+    copies = [
+        pltpu.make_async_copy(
+            far.at[pl.ds(i * size, size)], near.at[pl.ds(i * size, size)], sems.at[part, i]
+        )
+        for part, (far, near) in enumerate(((far_re_ref, re_ref), (far_im_ref, im_ref)))
+        for i in range(count)
+    ]
+    for copy in copies + small:
+        copy.start()
+    for copy in copies + small:
+        copy.wait()
+    count = map_ref.shape[0]
+    lines = place_ref.shape[0] // 2
+    small_ref[0:count, :] = map_ref[...]
+    small_ref[count : count + lines, :] = jnp.concatenate(
+        [place_ref[0:lines, :], place_ref[lines:, :]], 1
+    )
+    small_ref[count + lines :, :] = jnp.concatenate(
+        [
+            sites_ref[:, 0 : small_ref.shape[1]],
+            sites_ref[:, small_ref.shape[1] :],
+            jnp.zeros((2, small_ref.shape[1]), jnp.int32),
+        ],
+        0,
+    )
     rows = re_ref.shape[0] // 2
     bands = send_ref.shape[0]
 
@@ -108,21 +182,32 @@
         send_ref[band, 4:8, :] = packed[4 * band : 4 * band + 4, :]
 
 
-def phase_kernel(grid, columns, map_ref, place_ref, sites_ref, phase_ref):
-    atoms = sites_ref.shape[0]
-    groups, rows = map_ref.shape
-    sites = sites_ref[...].astype(bf16)
-    column_x = place_ref[:, 0:1].astype(f32)
-    column_y = place_ref[:, 1:2].astype(f32)
+def phase_kernel(grid, columns, small_ref, far_ref, phase_ref, sems):
+    groups, _, rows = phase_ref.shape
+    atoms = phase_ref.shape[1] // 2
+    sites = jnp.concatenate([small_ref[16:19, :], small_ref[19:22, :]], 1).astype(f32)
+    sites = jnp.concatenate([sites, jnp.zeros((5, atoms), f32)], 0).astype(bf16)
+    owner = lax.axis_index("pw")
+    packs = rows // columns
+    row = lax.div(owner, packs // 2)
+    line = small_ref[pl.ds(groups + lax.rem(row, groups), 1), :]
+    block = lax.div(row, groups) * (packs // 2) + lax.rem(owner, packs // 2)
+    mine = jnp.zeros((1, columns), jnp.int32)
+    for j in range(packs):
+        chosen = (block == j).astype(jnp.int32)
+        mine = mine + chosen * line[:, j * columns : (j + 1) * columns]
+    mine = jnp.concatenate([mine, jnp.zeros((7, columns), jnp.int32)], 0).T[:, 0:1]
+    column_x = lax.div(mine, grid).astype(f32)
+    column_y = lax.rem(mine, grid).astype(f32)
     ticks = lax.broadcasted_iota(jnp.int32, (columns, rows), 0)
     for s in range(groups):
-        cell = map_ref[s : s + 1, :]
+        cell = small_ref[s : s + 1, :]
         depth = lax.div(cell, columns).astype(f32)
         hot = ticks == lax.rem(cell, columns)
         x = jnp.sum(jnp.where(hot, column_x, 0.0), 0, keepdims=True)
         y = jnp.sum(jnp.where(hot, column_y, 0.0), 0, keepdims=True)
         place = jnp.concatenate([depth, x, y, jnp.zeros((5, rows), f32)], 0).astype(bf16)
-        turns = dot(sites, place)
+        turns = dot(sites, place, 0, 0)
         turns = turns - grid * jnp.floor(turns * (1.0 / grid) + 0.5)
         u = turns * (1.0 / grid)
         w = u * u
@@ -134,17 +219,37 @@
             h = h * w + SIN_POLY[k]
         h = h * u
         twice = h + h
-        phase_ref[0:atoms, s * rows : (s + 1) * rows] = (1.0 - twice * h).astype(bf16)
-        phase_ref[atoms : 2 * atoms, s * rows : (s + 1) * rows] = (twice * c).astype(bf16)
+        phase_ref[s, 0:atoms, :] = (1.0 - twice * h).astype(bf16)
+        phase_ref[s, atoms : 2 * atoms, :] = (twice * c).astype(bf16)
+        pltpu.make_async_copy(phase_ref.at[s], far_ref.at[s], sems.at[s]).start()
+    for s in range(groups):
+        pltpu.make_async_copy(phase_ref.at[s], far_ref.at[s], sems.at[s]).wait()
 
 
 def two_rows(ref, s, line):
     return jnp.concatenate([ref[s, line : line + 1, :], ref[s, line + 1 : line + 2, :]], 1)
 
 
-def columns_kernel(columns, map_ref, form_ref, phase_ref, table_ref, got_ref, send_ref):
-    groups, rows = map_ref.shape
-    atoms = phase_ref.shape[0] // 2
+def make_copies(far_ref, near_ref, sems):
+    return [
+        pltpu.make_async_copy(far_ref.at[i], near_ref.at[i], sems.at[i])
+        for i in range(near_ref.shape[0])
+    ]
+
+
+def fetch(far_ref, near_ref, sems):
+    copies = make_copies(far_ref, near_ref, sems)
+    for copy in copies:
+        copy.start()
+    return copies
+
+
+def columns_kernel(
+    columns, small_ref, form_ref, far_ref, table_ref, got_ref, send_ref, phase_ref, sems
+):
+    copies = fetch(far_ref, phase_ref, sems)
+    groups, _, rows = phase_ref.shape
+    atoms = phase_ref.shape[1] // 2
     grid = table_ref.shape[1]
     planes = send_ref.shape[1]
     owners = send_ref.shape[0]
@@ -156,7 +261,7 @@
     for s in range(groups):
         psi_re = two_rows(got_ref, s, 0)
         psi_im = two_rows(got_ref, s, 2)
-        cell = map_ref[s : s + 1, :]
+        cell = small_ref[s : s + 1, :]
         depth_hot = (deep == lax.div(cell, columns)).astype(f32).astype(bf16)
         hot = ticks == lax.rem(cell, columns)
         spread = jnp.concatenate([jnp.where(hot, psi_re, 0.0), jnp.where(hot, psi_im, 0.0)], 0)
@@ -171,9 +276,13 @@
     by_sin = dot3((table_ref[2], table_ref[3]), column, 1, 1)
     deep_re = by_cos[:, :columns] - by_sin[:, columns:]
     deep_im = by_sin[:, :columns] + by_cos[:, columns:]
-    products = dot(phase_ref[0:atoms, :], jnp.concatenate(first, 1), 1, 1) + dot(
-        phase_ref[atoms : 2 * atoms, :], jnp.concatenate(second, 1), 1, 1
-    )
+    products = jnp.zeros((atoms, 2 * channels), f32)
+    for s in range(groups):
+        copies[s].wait()
+        products = products + (
+            dot(phase_ref[s, 0:atoms, :], first[s], 1, 1)
+            + dot(phase_ref[s, atoms : 2 * atoms, :], second[s], 1, 1)
+        )
     parts = [products[owners * k : owners * (k + 1)] for k in range(atoms // owners)]
     half = len(parts) // 2
     overlap = jnp.sum(got_ref[:, 4:8, :], 0).T
@@ -190,80 +299,186 @@
         send_ref[:, k, :] = jnp.concatenate([deep_re[lines], deep_im[lines], extra[k]], 1)
 
 
-def planes_kernel(columns, place_ref, pot_ref, table_ref, got_ref, send_ref):
+def fold_kernel(pot_ref, out_ref):
     planes, grid, _ = pot_ref.shape
+
+    def chooser(size):
+        half = size // 2
+        line = lax.broadcasted_iota(jnp.int32, (size, grid), 0)
+        spot = lax.broadcasted_iota(jnp.int32, (size, grid), 1)
+        t = jnp.where(line < half, line, line - half)
+        plus = (line < half) & (t <= grid // 2) & (spot == t)
+        minus = (line >= half) & (t > 0) & (t < grid // 2) & (spot == grid - t)
+        return jnp.where(plus | minus, 1.0, 0.0).astype(bf16)
+
+    lines = chooser(out_ref.shape[1])
+    spots = chooser(out_ref.shape[2])
+    for k in range(planes):
+        part = sum(dot(lines, piece) for piece in split3(pot_ref[k]))
+        part = sum(dot(piece, spots, 1, 1) for piece in split3(part))
+        out_ref[k] = part * (1.0 / grid**3)
+
+
+def planes_kernel(
+    columns,
+    grid,
+    small_ref,
+    fold_ref,
+    table_x_ref,
+    table_y_ref,
+    far_ref,
+    got_ref,
+    send_ref,
+    phase_ref,
+    sems,
+    value_ref,
+    place_ref,
+    hot_ref,
+    field_ref,
+):
+    planes, size_x, size_y = fold_ref.shape
+    half_x, half_y = size_x // 2, size_y // 2
     owners = got_ref.shape[0]
-    steps, lanes = place_ref.shape[1:]
-    packs = lanes // owners
-    ticks = lax.broadcasted_iota(jnp.int32, (grid, lanes), 0)
-    cos = (table_ref[0], table_ref[1])
-    sin = (table_ref[2], table_ref[3])
-    values = []
-    for k in range(planes):
-        turned = got_ref[:, k, :].T
-        for part in range(2):
-            high, low = split(stripes(turned[part * columns : (part + 1) * columns], packs))
-            values.append((high.astype(f32), low.astype(f32)))
-    field = jnp.zeros((2 * planes * grid, grid), f32)
-    hots = []
-    for q in range(steps):
-        hot_x = ticks == place_ref[0, q : q + 1, :]
-        hot_y = (ticks == place_ref[1, q : q + 1, :]).astype(f32).astype(bf16)
-        hots.append((hot_x, hot_y))
-        for piece in range(2):
-            spread = jnp.concatenate(
-                [jnp.where(hot_x, v[piece][q : q + 1, :], 0.0).astype(bf16) for v in values], 0
-            )
-            field = field + dot(spread, hot_y, 1, 1)
-
-    def along_y(parts):
-        pieces = split(jnp.concatenate(parts, 0))
-        return dot3(pieces, cos), dot3(pieces, sin)
-
-    parts = [field[i * grid : (i + 1) * grid] for i in range(2 * planes)]
-    by_cos, by_sin = along_y(parts)
-    back = []
-    for k in range(planes):
-        re = slice(2 * k * grid, (2 * k + 1) * grid)
-        im = slice((2 * k + 1) * grid, (2 * k + 2) * grid)
-        now_re = split(by_cos[re] - by_sin[im])
-        now_im = split(by_sin[re] + by_cos[im])
-        real = dot3(cos, now_re) - dot3(sin, now_im)
-        imag = dot3(sin, now_re) + dot3(cos, now_im)
-        scaled = pot_ref[k] * (1.0 / grid**3)
-        real = split(real * scaled)
-        imag = split(imag * scaled)
-        back.append(dot3(cos, real) + dot3(sin, imag))
-        back.append(dot3(cos, imag) - dot3(sin, real))
-    by_cos, by_sin = along_y(back)
-    final = []
-    for k in range(planes):
-        re = slice(2 * k * grid, (2 * k + 1) * grid)
-        im = slice((2 * k + 1) * grid, (2 * k + 2) * grid)
-        final.append(by_cos[re] + by_sin[im])
-        final.append(by_cos[im] - by_sin[re])
-    high, low = split(jnp.concatenate(final, 0))
-    found = [[] for _ in final]
-    for q in range(steps):
-        hot_x, hot_y = hots[q]
-        mixed = dot(high, hot_y) + dot(low, hot_y)
-        for i in range(2 * planes):
-            picked = jnp.where(hot_x, mixed[i * grid : (i + 1) * grid], 0.0)
-            found[i].append(jnp.sum(picked, 0, keepdims=True))
-    for k in range(planes):
-        halves = [unstripe(jnp.concatenate(found[2 * k + i], 0), packs) for i in range(2)]
-        turned = jnp.concatenate(halves, 0).T
-        ride = jnp.sum(got_ref[:, k, 2 * columns :], 0, keepdims=True)
-        send_ref[:, k, :] = jnp.concatenate(
-            [turned, jnp.broadcast_to(ride, (owners, ride.shape[1]))], 1
+    steps, _, wide = phase_ref.shape
+    lines, lanes = 2 * steps, wide // 2
+    packs = lanes // columns
+    ticks_x = lax.broadcasted_iota(jnp.int32, (half_x, wide), 0)
+    ticks_y = lax.broadcasted_iota(jnp.int32, (half_y, wide), 0)
+    count = 2 * planes
+
+    def folded(at):
+        t = jnp.minimum(at, grid - at)
+        sign = jnp.where(at == t, 1.0, -1.0)
+        return t.astype(f32), jnp.where((t == 0) | (2 * t == grid), 0.0, sign)
+
+    def along_y(part):
+        high, low = split(part)
+        return dot(jnp.concatenate([high, low, high], 1), table_y_ref[...])
+
+    def along_x(part):
+        high, low = split(part)
+        return dot(table_x_ref[...], jnp.concatenate([high, high, low], 0))
+
+    def quarters(part):
+        return (
+            part[:half_x, :half_y],
+            part[:half_x, half_y:],
+            part[half_x:, :half_y],
+            part[half_x:, half_y:],
         )
 
+    def join(ee, eo, oe, oo):
+        return jnp.concatenate(
+            [jnp.concatenate([ee, eo], 1), jnp.concatenate([oe, oo], 1)], 0
+        )
+
+    step = pl.program_id(0)
+
+    @pl.when(step == 0)
+    def to_planes():
+        fetch(far_ref, phase_ref, sems)
+        place = small_ref[steps : 2 * steps, :]
+        for i, at in enumerate((lax.div(place, grid), lax.rem(place, grid))):
+            place_ref[2 * i], place_ref[2 * i + 1] = folded(at)
+        for k in range(planes):
+            loaded = [got_ref[pl.ds(j, lines, stride=packs), k, :] for j in range(packs)]
+            for part in range(2):
+                spot = slice(part * columns, (part + 1) * columns)
+                value = jnp.concatenate([v[:, spot] for v in loaded], 1)
+                value = jnp.concatenate([value[:steps], value[steps:]], 1)
+                for piece, half in enumerate(split(value)):
+                    half = half.astype(f32)
+                    value_ref[piece, 2 * (2 * k + part)] = half
+                    value_ref[piece, 2 * (2 * k + part) + 1] = half * place_ref[1]
+        field = jnp.zeros((count * size_x, size_y), f32)
+        for q in range(steps):
+            hot_x = ticks_x == place_ref[0, q : q + 1, :].astype(jnp.int32)
+            hot_y = ticks_y == place_ref[2, q : q + 1, :].astype(jnp.int32)
+            hot_y = jnp.concatenate(
+                [jnp.where(hot_y, 1.0, 0.0), jnp.where(hot_y, place_ref[3, q : q + 1, :], 0.0)], 0
+            ).astype(bf16)
+            hot_ref[q] = hot_y
+            for piece in range(2):
+                spread = [
+                    jnp.where(hot_x, value_ref[piece, i, q : q + 1, :], 0.0) for i in range(2 * count)
+                ]
+                field = field + dot(jnp.concatenate(spread, 0).astype(bf16), hot_y, 1, 1)
+        field_ref[...] = field
+
+    @pl.when(step == 1)
+    def transforms():
+        field = along_y(field_ref[...])
+        back = []
+        for k in range(planes):
+            re, im = [
+                quarters(along_x(field[(2 * k + i) * size_x : (2 * k + i + 1) * size_x]))
+                for i in range(2)
+            ]
+            values_v = quarters(fold_ref[k])
+            real_sum, real_gap = re[0] - re[3], re[0] + re[3]
+            imag_sum, imag_gap = im[0] - im[3], im[0] + im[3]
+            cross_re, cross_re_gap = re[1] + re[2], re[1] - re[2]
+            cross_im, cross_im_gap = im[1] + im[2], im[1] - im[2]
+            pp_re, mm_re = real_sum - cross_im, real_sum + cross_im
+            pp_im, mm_im = imag_sum + cross_re, imag_sum - cross_re
+            pm_re, mp_re = real_gap + cross_im_gap, real_gap - cross_im_gap
+            pm_im, mp_im = imag_gap - cross_re_gap, imag_gap + cross_re_gap
+            parts = []
+            for pp, pm, mp, mm in (
+                (pp_re, pm_re, mp_re, mm_re),
+                (pp_im, pm_im, mp_im, mm_im),
+            ):
+                pp, pm, mp, mm = [a * b for a, b in zip((pp, pm, mp, mm), values_v)]
+                plus_s, plus_g = pp + pm, pp - pm
+                minus_s, minus_g = mp + mm, mp - mm
+                parts.append((plus_s + minus_s, plus_g + minus_g, plus_s - minus_s, plus_g - minus_g))
+            re, im = parts
+            back.append(along_x(join(re[0], im[1], im[2], -re[3])))
+            back.append(along_x(join(im[0], -re[1], -re[2], -im[3])))
+        field_ref[...] = along_y(jnp.concatenate(back, 0))
+
+    @pl.when(step == 2)
+    def to_columns():
+        high, low = split(field_ref[...])
+        for q in range(steps):
+            hot_x = ticks_x == place_ref[0, q : q + 1, :].astype(jnp.int32)
+            sign_x = place_ref[1, q : q + 1, :]
+            hot_y = hot_ref[q]
+            mixed = dot(high, hot_y) + dot(low, hot_y)
+            for i in range(count):
+                even = mixed[i * size_x : i * size_x + half_x]
+                odd = mixed[i * size_x + half_x : (i + 1) * size_x]
+                picked = jnp.where(hot_x, even + sign_x * odd, 0.0)
+                value_ref[0, i, q : q + 1, :] = jnp.sum(picked, 0, keepdims=True)
+        for k in range(planes):
+            halves = [value_ref[0, 2 * k + i] for i in range(2)]
+            halves = [jnp.concatenate([v[:, :lanes], v[:, lanes:]], 0) for v in halves]
+            ride = jnp.sum(got_ref[:, k, 2 * columns :], 0, keepdims=True)
+            ride = jnp.broadcast_to(ride, (lines, ride.shape[1]))
+            for j in range(packs):
+                spot = slice(j * columns, (j + 1) * columns)
+                send_ref[pl.ds(j, lines, stride=packs), k, :] = jnp.concatenate(
+                    [halves[0][:, spot], halves[1][:, spot], ride], 1
+                )
+        for copy in make_copies(far_ref, phase_ref, sems):
+            copy.wait()
+
 
 def image_kernel(
-    columns, waves, map_ref, form_ref, kinetic_ref, strength_ref, phase_ref, table_ref, psi_ref, got_ref, send_ref
+    columns,
+    waves,
+    small_ref,
+    form_ref,
+    kinetic_ref,
+    strength_ref,
+    phase_ref,
+    table_ref,
+    psi_ref,
+    got_ref,
+    send_ref,
 ):
-    groups, rows = map_ref.shape
-    atoms = phase_ref.shape[0] // 2
+    groups, _, rows = phase_ref.shape
+    atoms = phase_ref.shape[1] // 2
     grid = table_ref.shape[1]
     owners, planes, _ = got_ref.shape
     channels = form_ref.shape[0]
@@ -275,13 +490,16 @@
     sums = jnp.concatenate(
         [r[:, wide * i : wide * (i + 1)] for r in ride[:2] for i in range(per_row)], 0
     ).T
-    factor = jnp.concatenate([strength_ref[...], strength_ref[...]], 0)
+    line = lax.broadcasted_iota(jnp.int32, (wide, channels), 0)
+    spot = lax.broadcasted_iota(jnp.int32, (wide, channels), 1)
+    factor = jnp.sum(
+        jnp.where(lax.rem(line, channels) == spot, strength_ref[...], 0.0), 1, keepdims=True
+    )
     scaled = factor * (sums / root) / root
     scaled_re = scaled[:channels].astype(bf16)
     scaled_im = scaled[channels:].astype(bf16)
-    mixed = dot(jnp.concatenate([scaled_re, scaled_im], 0), phase_ref[0:atoms, :]) + dot(
-        jnp.concatenate([scaled_im, -scaled_re], 0), phase_ref[atoms : 2 * atoms, :]
-    )
+    first = jnp.concatenate([scaled_re, scaled_im], 0)
+    second = jnp.concatenate([scaled_im, -scaled_re], 0)
     deep = split(jnp.concatenate([g[:, : 2 * columns] for g in got], 0).T)
     by_cos = dot3(deep, (table_ref[0], table_ref[1]))
     by_sin = dot3(deep, (table_ref[2], table_ref[3]))
@@ -292,7 +510,7 @@
     depths = lax.broadcasted_iota(jnp.int32, (grid, rows), 0)
     overlap = jnp.concatenate([ride[2][:, 0:4].T, ride[2][:, 4:8].T], 1)
     for s in range(groups):
-        cell = map_ref[s : s + 1, :]
+        cell = small_ref[s : s + 1, :]
         depth_hot = (depths == lax.div(cell, columns)).astype(f32).astype(bf16)
         hot = ticks == lax.rem(cell, columns)
         found = dot(out, depth_hot)
@@ -300,9 +518,11 @@
         local_re = jnp.sum(jnp.where(hot, found[:columns], 0.0), 0, keepdims=True)
         local_im = jnp.sum(jnp.where(hot, found[columns:], 0.0), 0, keepdims=True)
         form = form_ref[:, s, :]
-        lanes = slice(s * rows, (s + 1) * rows)
-        near_re = jnp.sum(form * mixed[:channels, lanes], 0, keepdims=True)
-        near_im = jnp.sum(form * mixed[channels:, lanes], 0, keepdims=True)
+        mixed = dot(first, phase_ref[s, 0:atoms, :]) + dot(
+            second, phase_ref[s, atoms : 2 * atoms, :]
+        )
+        near_re = jnp.sum(form * mixed[:channels], 0, keepdims=True)
+        near_im = jnp.sum(form * mixed[channels:], 0, keepdims=True)
         kinetic = kinetic_ref[s : s + 1, :]
         image_re = kinetic * two_rows(psi_ref, s, 0) + local_re + near_re
         image_im = kinetic * two_rows(psi_ref, s, 2) + local_im + near_im
@@ -434,62 +654,103 @@
     waves = band_count * owners * row_count
     atoms = atom_sites.shape[1]
     rows = blocks * slab
-    flat_table, owner_table = transform_tables(grid, planes)
-    flat_table = jnp.asarray(flat_table)
-    owner_table = jnp.asarray(owner_table)
-
-    def exchange(part, axis):
-        return lax.all_to_all(part, axis, split_axis=0, concat_axis=0, tiled=True)
-
-    basis, send = kernel_call(
+    half_x, half_y = grid // 2 + 8, 128
+    tables = transform_tables(grid, planes, half_x, half_y)
+    owner_table, table_x, table_y = [jnp.asarray(table) for table in tables]
+
+    def exchange(part, axis, groups=None):
+        return lax.all_to_all(
+            part, axis, split_axis=0, concat_axis=0, axis_index_groups=groups, tiled=True
+        )
+
+    near, far = {}, {}
+    for z in range(band_count):
+        for p in range(owners):
+            y, rest = divmod(p, 8)
+            near.setdefault((z // 2, y // 2), []).append(z * owners + p)
+            far.setdefault((z % 2, y % 2, rest), []).append(z * owners + p)
+    near, far = list(near.values()), list(far.values())
+
+    places = column_map.reshape(-1, 128)
+    basis, send, small = kernel_call(
         pack_kernel,
-        (shape(2 * rows, row_count), shape(slab, 8, 128)),
+        (
+            shape(2 * rows, row_count),
+            shape(slab, 8, 128),
+            shape(3 * 8, row_count, dtype=jnp.int32),
+        ),
         basis_re.reshape(-1, 128),
         basis_im.reshape(-1, 128),
+        sphere_map,
+        places,
+        atom_sites,
+        scratch=(
+            pltpu.VMEM((2 * rows, 128), f32),
+            pltpu.VMEM((2 * rows, 128), f32),
+            pltpu.VMEM(sphere_map.shape, jnp.int32),
+            pltpu.VMEM(places.shape, jnp.int32),
+            pltpu.VMEM(atom_sites.shape, jnp.int32),
+            pltpu.SemaphoreType.DMA((2, 4)),
+            pltpu.SemaphoreType.DMA((3,)),
+        ),
+        far=(0, 1, 2, 3, 4),
+        vmem=63,
     )
     psi = exchange(send, "band")
 
-    x_index = column_map // grid
-    y_index = column_map % grid
-    both = jnp.stack([x_index, y_index])
-    mine = lax.dynamic_slice_in_dim(both, lax.axis_index("pw") * columns, columns, 1).T
-    spread = both.reshape(2, owners, columns // 8, 8).transpose(0, 3, 2, 1).reshape(2, 8, -1)
-    sites = jnp.pad(atom_sites, ((0, 5), (0, 0))).T.astype(f32)
-    phase = kernel_call(
+    phase_dims = (band_count, 2 * atoms, row_count)
+    phase_sems = (pltpu.SemaphoreType.DMA((band_count,)),)
+    phase_scratch = (pltpu.VMEM(phase_dims, bf16),) + phase_sems
+    far_phase = kernel_call(
         lambda *refs: phase_kernel(grid, columns, *refs),
-        shape(2 * atoms, band_count * row_count, dtype=bf16),
-        sphere_map,
-        mine,
-        sites,
+        shape(16 * band_count, *phase_dims[1:], dtype=bf16),
+        small,
+        scratch=phase_scratch,
+        far_out=(0,),
+        vmem=8,
         flops=10**7,
     )
     send = kernel_call(
         lambda *refs: columns_kernel(columns, *refs),
         shape(owners, planes, 128),
-        sphere_map,
+        small,
         form_factors,
-        phase,
+        far_phase,
         owner_table,
         psi,
+        scratch=phase_scratch,
+        far=(2,),
     )
     got = exchange(send, "pw")
-    send = kernel_call(
-        lambda *refs: planes_kernel(columns, *refs),
-        shape(owners, planes, 128),
-        spread,
-        potential,
-        flat_table,
+    folded = kernel_call(fold_kernel, shape(planes, 2 * half_x, 2 * half_y), potential)
+    send, phase = kernel_call(
+        lambda *refs: planes_kernel(columns, grid, *refs),
+        (shape(owners, planes, 128), shape(*phase_dims, dtype=bf16)),
+        small,
+        folded,
+        table_x,
+        table_y,
+        far_phase,
         got,
-        vmem=48,
+        scratch=phase_sems
+        + (
+            pltpu.VMEM((2, 4 * planes, 8, row_count), f32),
+            pltpu.VMEM((4, 8, row_count), f32),
+            pltpu.VMEM((8, 2 * half_y, row_count), bf16),
+            pltpu.VMEM((4 * planes * half_x, 2 * half_y), f32),
+        ),
+        grid=(3,),
+        far=(4,),
+        vmem=16,
     )
     got = exchange(send, "pw")
     send = kernel_call(
         lambda *refs: image_kernel(columns, waves, *refs),
         shape(band_count, 8, 128),
-        sphere_map,
+        small,
         form_factors,
         kinetic,
-        channel_strength[:, None],
+        channel_strength[None, :],
         phase,
         owner_table,
         psi,
@@ -498,16 +759,16 @@
     got = exchange(send, "band")
     image, send = kernel_call(
         lambda *refs: products_kernel(waves, *refs),
-        (shape(2 * slab, row_count), shape(owners, 1, 9 * 128)),
+        (shape(2 * slab, row_count), shape(len(near[0]), 1, 9 * 128)),
         basis,
         got,
     )
     over = kernel_call(
         lambda *refs: overlap_kernel(waves, *refs), shape(2 * rows, 2 * rows), got
     )
-    got = exchange(send, "pw")
-    send = kernel_call(gather_kernel, shape(band_count, 1, 9 * 128), got)
-    got = exchange(send, "band")
+    got = exchange(send, ("band", "pw"), near)
+    send = kernel_call(gather_kernel, shape(len(far[0]), 1, 9 * 128), got)
+    got = exchange(send, ("band", "pw"), far)
     next_re, next_im, coef_re, coef_im, chol_re, chol_im = kernel_call(
         finish_kernel,
         (

time: 132 us -> 117 us (0.89)
  local copies, waits for them, and re-layouts: 10.4 us -> 0.78 us
  waiting for transfers between devices: 28.3 us -> 21.7 us
  blocking collectives: 32.5 us -> 38.9 us
  starting transfers between devices: 29.7 us -> 26.6 us
    unnamed x28 -> x20, local copies, waits for them, and re-layouts: 9.69 us -> 0.78 us
    all_to_all x4 -> x3, waiting for transfers between devices: 28.3 us -> 21.7 us  [exchange(): lax.all_to_all(part, axis, split_axis=0, concat_axis=0, axis_index_groups...]
    all_to_all x2 -> x3, blocking collectives: 32.5 us -> 38.9 us  [exchange(): lax.all_to_all(part, axis, split_axis=0, concat_axis=0, axis_index_groups...]
    all_to_all x4 -> x3, starting transfers between devices: 29.7 us -> 26.6 us  [exchange(): lax.all_to_all(part, axis, split_axis=0, concat_axis=0, axis_index_groups...]
    pallas_call x9 -> x10, Pallas kernels: 29.1 us -> 28.2 us  [kernel_call(): pl.pallas_call(kernel, out_shape=outs, in_specs=[place[i in far] for i in...]
  transfers between devices with their start and end apart: 4 -> 3, of which waited for: 3 -> 3; matrix products, arithmetic and copies ran while one was open for 2% -> 0% of each run, Pallas kernels for 3% -> 6%
where the time goes in v2:
time: 117 us
  blocking collectives  38.9 us (33%)
  Pallas kernels  28.2 us (24%)
  starting transfers between devices  26.6 us (23%)
  waiting for transfers between devices  21.7 us (19%)
    all_to_all x3, blocking collectives, exchange(): lax.all_to_all(part, axis, split_axis=0, concat_axis=0, axis_index_groups...  38.9 us
    pallas_call x10, Pallas kernels, kernel_call(): pl.pallas_call(kernel, out_shape=outs, in_specs=[place[i in far] for i in...  28.2 us
    all_to_all x3, starting transfers between devices, exchange(): lax.all_to_all(part, axis, split_axis=0, concat_axis=0, axis_index_groups...  26.6 us
    all_to_all x3, waiting for transfers between devices, exchange(): lax.all_to_all(part, axis, split_axis=0, concat_axis=0, axis_index_groups...  21.7 us
  transfers between devices with their start and end apart: 3, of which 3 were waited for; matrix products, arithmetic and copies ran while one was open for 0% of the time, Pallas kernels for 6%

profile of v2, /device:TPU:1, one launch (start us, length us, event | category | flops | bytes accessed | tf_op | source)
XLA Modules:
  0.0 117.0 jit_solution(13453879506764411960)
XLA Ops:
  0.6 0.0 copy-start
  0.6 2.1 %shard_map.163 = (f32[128,256]{1,0:T(8,128)}, f32[8,8,128]{2,1,0:T(8,128)}, s32[24,256]{1,0:T(8,128)}) custom-call(f32[128,128]{1,0:T(8,128)} %bitcast.9, f32[128,128]{1,0:T(8,128)} %bitcast.10, s32[8,256]{1,0:T(8,128)} %far_map_ref.1, s32[16,128]{1,0:T(8,128)} %bitcast.11, s32[3,512]{1,0:T(4,128)} %far_sites_ref.1), custom_call_target="tpu_custom_call" | custom-call | flops 1000000 | bytes 4000000 | tf_op jit(solution)/shard_map/pallas_call | solution.py:95
  2.7 10.9 %all-to-all-start = ((f32[8,8,128]{2,1,0:T(8,128)}), f32[8,8,128]{2,1,0:T(8,128)S(1)}, u32[]{:S(2)}, u32[]{:S(2)}) async-start(f32[8,8,128]{2,1,0:T(8,128)} %get-tuple-element.21), calls=%async_computation | async-start | bytes 65536 | tf_op jit(solution)/shard_map/all_to_all | solution.py:662
  13.6 0.7 copy-done.3
  14.4 0.0 copy-start.6
  14.4 5.6 %shard_map.165.refs_2_.refs_4_ = bf16[128,1024,256]{2,1,0:T(8,128)(2,1)} custom-call(s32[24,256]{1,0:T(8,128)S(1)} %copy-done.3), custom_call_target="tpu_custom_call" | custom-call | flops 10000000 | bytes 4000000 | tf_op jit(solution)/shard_map/pallas_call | solution.py:95
  20.0 0.0 copy-start.8
  20.0 0.0 copy-start.9
  20.0 0.0 copy-start.2
  20.0 0.5 all-to-all-done.refs_4_.refs_6_
  20.5 0.0 copy-done
  20.5 0.0 copy-done.7
  20.5 5.1 %shard_map.166 = f32[64,3,128]{2,1,0:T(4,128)} custom-call(s32[24,256]{1,0:T(8,128)S(1)} %copy-done.3, f32[8,8,256]{2,1,0:T(8,128)S(1)} %copy-done.7, bf16[128,1024,256]{2,1,0:T(8,128)(2,1)} %shard_map.165.refs_2_.refs_4_, bf16[4,192,192]{2,1,0:T(8,128)(2,1)S(1)} %copy-done, f32[8,8,128]{2,1,0:T(8,128)S(1)} %all-to-all-done.refs_4_.refs_6_), custom_call_target="tpu_custom_call" | custom-call | flops 1000000 | bytes 4000000 | tf_op jit(solution)/shard_map/pallas_call | solution.py:95
  25.6 12.2 %all-to-all-start.1 = ((f32[64,3,128]{2,1,0:T(4,128)}), f32[64,3,128]{2,1,0:T(4,128)S(1)}, u32[]{:S(2)}, u32[]{:S(2)}) async-start(f32[64,3,128]{2,1,0:T(4,128)} %shard_map.166), calls=%async_computation.1 | async-start | bytes 262144 | tf_op jit(solution)/shard_map/all_to_all | solution.py:662
  37.8 0.0 copy-done.1
  37.9 0.9 shard_map.164.refs_1_
  38.8 10.2 %all-to-all-done.1.refs_5_ = f32[64,3,128]{2,1,0:T(4,128)S(1)} async-done(((f32[64,3,128]{2,1,0:T(4,128)}), f32[64,3,128]{2,1,0:T(4,128)S(1)}, u32[]{:S(2)}, u32[]{:S(2)}) %all-to-all-start.1) | async-done | bytes 98336 | tf_op jit(solution)/shard_map/all_to_all | solution.py:662
  49.0 0.0 copy-done.4
  49.0 0.0 copy-done.5
  49.0 0.0 copy-done.6
  49.0 10.0 %shard_map.167 = (f32[64,3,128]{2,1,0:T(4,128)S(1)}, bf16[8,1024,256]{2,1,0:T(8,128)(2,1)S(1)}) custom-call(s32[24,256]{1,0:T(8,128)S(1)} %copy-done.4, f32[3,208,256]{2,1,0:T(8,128)S(1)} %shard_map.164.refs_1_, bf16[208,624]{1,0:T(8,128)(2,1)S(1)} %copy-done.6, bf16[768,256]{1,0:T(8,128)(2,1)S(1)} %copy-done.5, ...), custom_call_target="tpu_custom_call" | custom-call | flops 1000000 | bytes 4000000 | tf_op jit(solution)/shard_map/pallas_call | solution.py:95
  59.0 14.9 %all_to_all.30.refs_7_ = f32[64,3,128]{2,1,0:T(4,128)S(1)} all-to-all(f32[64,3,128]{2,1,0:T(4,128)S(1)} %get-tuple-element.23), channel_id=1, replica_groups=mesh['band'=8,'pw'=64] {'pw'}, dimensions={0} | all-to-all | bytes 196608 | tf_op jit(solution)/shard_map/all_to_all | solution.py:662
  73.9 0.0 copy-done.8
  73.9 1.2 %shard_map.168 = f32[8,8,128]{2,1,0:T(8,128)S(1)} custom-call(s32[24,256]{1,0:T(8,128)S(1)} %copy-done.4, f32[8,8,256]{2,1,0:T(8,128)S(1)} %copy-done.7, f32[8,256]{1,0:T(8,128)S(1)} %copy-done.8, f32[1,8]{1,0:T(1,128)S(1)} %bitcast.8, bf16[8,1024,256]{2,1,0:T(8,128)(2,1)S(1)} %get-tuple-element.22.refs_4_, bf16[4,192,192]{2,1,0:T(8,128)(2,1)S(1)} %copy-done, ...), custom_call_target="tpu_custom_call" | custom-call | flops 1000000 | bytes 4000000 | tf_op jit(solution)/shard_map/pallas_call | solution.py:95
  75.1 12.1 %all_to_all.31.refs_1_.refs_0_ = f32[8,8,128]{2,1,0:T(8,128)S(1)} all-to-all(f32[8,8,128]{2,1,0:T(8,128)S(1)} %shard_map.168), channel_id=1, replica_groups=mesh['band'=8,'pw'=64] {'band'}, dimensions={0} | all-to-all | bytes 65536 | tf_op jit(solution)/shard_map/all_to_all | solution.py:662
  87.2 0.5 shard_map.169
  87.7 11.9 %all_to_all.32.got_ref = f32[32,1,1152]{2,1,0:T(1,128)S(1)} all-to-all(f32[32,1,1152]{2,1,0:T(1,128)S(1)} %get-tuple-element.25), channel_id=1, replica_groups={{0,1,2,3,4,5,6,7,8,9,10,11,12,13,14,15,64,65,66,67,68,69,70,71,72,73,74..., dimensions={0} | all-to-all | bytes 294912 | tf_op jit(solution)/shard_map/all_to_all | solution.py:662
  99.6 0.7 shard_map.171
  100.3 3.5 %all-to-all-start.5 = ((f32[16,1,1152]{2,1,0:T(1,128)}), f32[16,1,1152]{2,1,0:T(1,128)S(1)}, u32[]{:S(2)}, u32[]{:S(2)}) async-start(f32[16,1,1152]{2,1,0:T(1,128)} %shard_map.171), calls=%async_computation.5 | async-start | bytes 147456 | tf_op jit(solution)/shard_map/all_to_all | solution.py:662
  103.8 0.2 shard_map.170.over_ref
  104.0 11.0 %all-to-all-done.5.got_ref = f32[16,1,1152]{2,1,0:T(1,128)S(1)} async-done(((f32[16,1,1152]{2,1,0:T(1,128)}), f32[16,1,1152]{2,1,0:T(1,128)S(1)}, u32[]{:S(2)}, u32[]{:S(2)}) %all-to-all-start.5) | async-done | bytes 73760 | tf_op jit(solution)/shard_map/all_to_all | solution.py:662
  115.1 1.9 %shard_map.172 = (f32[16,128]{1,0:T(8,128)}, f32[16,128]{1,0:T(8,128)}, f32[64,8]{1,0:T(8,128)}, f32[64,8]{1,0:T(8,128)}, f32[8,8]{1,0:T(8,128)}, /*index=5*/f32[8,8]{1,0:T(8,128)}) custom-call(f32[128,256]{1,0:T(8,128)S(1)} %copy-done.2, f32[16,256]{1,0:T(8,128)S(1)} %get-tuple-element.24.image_ref, f32[128,128]{1,0:T(8,128)S(1)} %shard_map.170.over_ref, ...), custom_call_target="tpu_custom_call" | custom-call | flops 1000000 | bytes 4000000 | tf_op jit(solution)/shard_map/pallas_call | solution.py:95
  (7 shorter events, 0.0 us)
Async XLA Ops:
  0.6 19.9 %copy-start = (bf16[4,192,192]{2,1,0:T(8,128)(2,1)S(1)}, bf16[4,192,192]{2,1,0:T(8,128)(2,1)}, u32[]{:S(2)}) copy-start(bf16[4,192,192]{2,1,0:T(8,128)(2,1)} %constant.6.clone.refs_3_.refs_5_) | copy-start | bytes 884740
  2.7 17.8 %all-to-all-start = ((f32[8,8,128]{2,1,0:T(8,128)}), f32[8,8,128]{2,1,0:T(8,128)S(1)}, u32[]{:S(2)}, u32[]{:S(2)}) async-start(f32[8,8,128]{2,1,0:T(8,128)} %get-tuple-element.21), calls=%async_computation | async-start | bytes 65536 | tf_op jit(solution)/shard_map/all_to_all | solution.py:662
  13.6 0.7 copy-start.3
  14.4 6.1 %copy-start.7 = (f32[8,8,256]{2,1,0:T(8,128)S(1)}, f32[8,8,256]{2,1,0:T(8,128)}, u32[]{:S(2)}) copy-start(f32[8,8,256]{2,1,0:T(8,128)} %refs_1_.3) | copy-start | bytes 196612
  14.4 23.5 %copy-start.1 = (f32[3,192,192]{2,1,0:T(8,128)S(1)}, f32[3,192,192]{2,1,0:T(8,128)}, u32[]{:S(2)}) copy-start(f32[3,192,192]{2,1,0:T(8,128)} %pot_ref.1) | copy-start | bytes 1327108
  14.4 34.6 %copy-start.4 = (s32[24,256]{1,0:T(8,128)S(1)}, s32[24,256]{1,0:T(8,128)}, u32[]{:S(2)}) copy-start(s32[24,256]{1,0:T(8,128)} %get-tuple-element.20.refs_0_) | copy-start | bytes 73732
  14.4 34.6 %copy-start.5 = (bf16[768,256]{1,0:T(8,128)(2,1)S(1)}, bf16[768,256]{1,0:T(8,128)(2,1)}, u32[]{:S(2)}) copy-start(bf16[768,256]{1,0:T(8,128)(2,1)} %constant.8.clone.refs_3_) | copy-start | bytes 1179652
  14.4 34.6 %copy-start.6 = (bf16[208,624]{1,0:T(8,128)(2,1)S(1)}, bf16[208,624]{1,0:T(8,128)(2,1)}, u32[]{:S(2)}) copy-start(bf16[208,624]{1,0:T(8,128)(2,1)} %constant.7.clone.refs_2_) | copy-start | bytes 778756
  20.0 53.9 %copy-start.8 = (f32[8,256]{1,0:T(8,128)S(1)}, f32[8,256]{1,0:T(8,128)}, u32[]{:S(2)}) copy-start(f32[8,256]{1,0:T(8,128)} %refs_2_.2) | copy-start | bytes 24580
  20.0 53.9 %copy-start.9 = (f32[8]{0:T(128)S(1)}, f32[8]{0:T(128)}, u32[]{:S(2)}) copy-start(f32[8]{0:T(128)} %param.17) | copy-start | bytes 100
  20.0 67.2 %copy-start.2 = (f32[128,256]{1,0:T(8,128)S(1)}, f32[128,256]{1,0:T(8,128)}, u32[]{:S(2)}) copy-start(f32[128,256]{1,0:T(8,128)} %get-tuple-element.19.refs_0_.basis_ref) | copy-start | bytes 393220
  25.6 23.4 %all-to-all-start.1 = ((f32[64,3,128]{2,1,0:T(4,128)}), f32[64,3,128]{2,1,0:T(4,128)S(1)}, u32[]{:S(2)}, u32[]{:S(2)}) async-start(f32[64,3,128]{2,1,0:T(4,128)} %shard_map.166), calls=%async_computation.1 | async-start | bytes 262144 | tf_op jit(solution)/shard_map/all_to_all | solution.py:662
  100.3 14.8 %all-to-all-start.5 = ((f32[16,1,1152]{2,1,0:T(1,128)}), f32[16,1,1152]{2,1,0:T(1,128)S(1)}, u32[]{:S(2)}, u32[]{:S(2)}) async-start(f32[16,1,1152]{2,1,0:T(1,128)} %shard_map.171), calls=%async_computation.5 | async-start | bytes 147456 | tf_op jit(solution)/shard_map/all_to_all | solution.py:662

commit v3 on v2

--- a/solution.py
+++ b/solution.py
@@ -13,7 +13,8 @@
 exact_mode = lax.Precision.HIGHEST
 
 COS_POLY = (0.9999999403953552, -4.934792995452881, 4.058411121368408, -1.331876516342163, 0.21968960762023926)
-SIN_POLY = (3.1415927410125732, -5.167710304260254, 2.550077438354492, -0.598291277885437, 0.07765766233205795)
+SIN_POLY = (3.1415903568267822, -5.1674065589904785, 2.5440104007720947, -0.5594624280929565)
+WHOLE = 1.5 * 2.0**23
 
 
 def dot(left, right, left_dim=1, right_dim=0, precision=None):
@@ -185,6 +186,12 @@
 def phase_kernel(grid, columns, small_ref, far_ref, phase_ref, sems):
     groups, _, rows = phase_ref.shape
     atoms = phase_ref.shape[1] // 2
+    copies = [
+        pltpu.make_async_copy(phase_ref.at[s], far_ref.at[s], sems.at[s]) for s in range(groups)
+    ]
+    root = math.sqrt(2.0)
+    cos_poly = [root * c / grid ** (2 * k) for k, c in enumerate(COS_POLY)]
+    sin_poly = [root * c / grid ** (2 * k + 1) for k, c in enumerate(SIN_POLY)]
     sites = jnp.concatenate([small_ref[16:19, :], small_ref[19:22, :]], 1).astype(f32)
     sites = jnp.concatenate([sites, jnp.zeros((5, atoms), f32)], 0).astype(bf16)
     owner = lax.axis_index("pw")
@@ -208,98 +215,41 @@
         y = jnp.sum(jnp.where(hot, column_y, 0.0), 0, keepdims=True)
         place = jnp.concatenate([depth, x, y, jnp.zeros((5, rows), f32)], 0).astype(bf16)
         turns = dot(sites, place, 0, 0)
-        turns = turns - grid * jnp.floor(turns * (1.0 / grid) + 0.5)
-        u = turns * (1.0 / grid)
-        w = u * u
-        c = COS_POLY[4]
-        for k in (3, 2, 1, 0):
-            c = c * w + COS_POLY[k]
-        h = SIN_POLY[4]
-        for k in (3, 2, 1, 0):
-            h = h * w + SIN_POLY[k]
-        h = h * u
-        twice = h + h
-        phase_ref[s, 0:atoms, :] = (1.0 - twice * h).astype(bf16)
-        phase_ref[s, atoms : 2 * atoms, :] = (twice * c).astype(bf16)
-        pltpu.make_async_copy(phase_ref.at[s], far_ref.at[s], sems.at[s]).start()
-    for s in range(groups):
-        pltpu.make_async_copy(phase_ref.at[s], far_ref.at[s], sems.at[s]).wait()
+        turns = turns - grid * ((turns * (1.0 / grid) + WHOLE) - WHOLE)
+        w = turns * turns
+        c = cos_poly[-1]
+        for value in cos_poly[-2::-1]:
+            c = c * w + value
+        h = sin_poly[-1]
+        for value in sin_poly[-2::-1]:
+            h = h * w + value
+        h = h * turns
+        phase_ref[s, 0:atoms, :] = (1.0 - h * h).astype(bf16)
+        phase_ref[s, atoms : 2 * atoms, :] = (h * c).astype(bf16)
+        copies[s].start()
+    for copy in copies:
+        copy.wait()
 
 
 def two_rows(ref, s, line):
     return jnp.concatenate([ref[s, line : line + 1, :], ref[s, line + 1 : line + 2, :]], 1)
 
 
-def make_copies(far_ref, near_ref, sems):
+def make_copies(far_ref, near_ref, sems, first=0):
     return [
-        pltpu.make_async_copy(far_ref.at[i], near_ref.at[i], sems.at[i])
+        pltpu.make_async_copy(far_ref.at[first + i], near_ref.at[i], sems.at[i])
         for i in range(near_ref.shape[0])
     ]
 
 
-def fetch(far_ref, near_ref, sems):
-    copies = make_copies(far_ref, near_ref, sems)
+def fetch(far_ref, near_ref, sems, first=0):
+    copies = make_copies(far_ref, near_ref, sems, first)
     for copy in copies:
         copy.start()
     return copies
 
 
-def columns_kernel(
-    columns, small_ref, form_ref, far_ref, table_ref, got_ref, send_ref, phase_ref, sems
-):
-    copies = fetch(far_ref, phase_ref, sems)
-    groups, _, rows = phase_ref.shape
-    atoms = phase_ref.shape[1] // 2
-    grid = table_ref.shape[1]
-    planes = send_ref.shape[1]
-    owners = send_ref.shape[0]
-    channels = form_ref.shape[0]
-    ticks = lax.broadcasted_iota(jnp.int32, (columns, rows), 0)
-    deep = lax.broadcasted_iota(jnp.int32, (grid, rows), 0)
-    total = jnp.zeros((4 * columns, grid), f32)
-    first, second = [], []
-    for s in range(groups):
-        psi_re = two_rows(got_ref, s, 0)
-        psi_im = two_rows(got_ref, s, 2)
-        cell = small_ref[s : s + 1, :]
-        depth_hot = (deep == lax.div(cell, columns)).astype(f32).astype(bf16)
-        hot = ticks == lax.rem(cell, columns)
-        spread = jnp.concatenate([jnp.where(hot, psi_re, 0.0), jnp.where(hot, psi_im, 0.0)], 0)
-        total = total + dot(jnp.concatenate(split(spread), 0), depth_hot, 1, 1)
-        form = form_ref[:, s, :]
-        weighted_re = (form * psi_re).astype(bf16)
-        weighted_im = (form * psi_im).astype(bf16)
-        first.append(jnp.concatenate([weighted_re, weighted_im], 0))
-        second.append(jnp.concatenate([-weighted_im, weighted_re], 0))
-    column = split(total[: 2 * columns] + total[2 * columns :])
-    by_cos = dot3((table_ref[0], table_ref[1]), column, 1, 1)
-    by_sin = dot3((table_ref[2], table_ref[3]), column, 1, 1)
-    deep_re = by_cos[:, :columns] - by_sin[:, columns:]
-    deep_im = by_sin[:, :columns] + by_cos[:, columns:]
-    products = jnp.zeros((atoms, 2 * channels), f32)
-    for s in range(groups):
-        copies[s].wait()
-        products = products + (
-            dot(phase_ref[s, 0:atoms, :], first[s], 1, 1)
-            + dot(phase_ref[s, atoms : 2 * atoms, :], second[s], 1, 1)
-        )
-    parts = [products[owners * k : owners * (k + 1)] for k in range(atoms // owners)]
-    half = len(parts) // 2
-    overlap = jnp.sum(got_ref[:, 4:8, :], 0).T
-    own = jnp.concatenate(
-        [overlap[:owners], overlap[owners:], jnp.zeros((owners, 2 * columns - 8), f32)], 1
-    )
-    extra = [
-        jnp.concatenate(parts[:half], 1),
-        jnp.concatenate(parts[half:], 1),
-        own,
-    ]
-    for k in range(planes):
-        lines = slice(owners * k, owners * (k + 1))
-        send_ref[:, k, :] = jnp.concatenate([deep_re[lines], deep_im[lines], extra[k]], 1)
-
-
-def fold_kernel(pot_ref, out_ref):
+def fold(pot_ref, out_ref):
     planes, grid, _ = pot_ref.shape
 
     def chooser(size):
@@ -314,9 +264,83 @@
     lines = chooser(out_ref.shape[1])
     spots = chooser(out_ref.shape[2])
     for k in range(planes):
-        part = sum(dot(lines, piece) for piece in split3(pot_ref[k]))
-        part = sum(dot(piece, spots, 1, 1) for piece in split3(part))
+        part = sum(dot(lines, piece) for piece in split(pot_ref[k]))
+        part = sum(dot(piece, spots, 1, 1) for piece in split(part))
         out_ref[k] = part * (1.0 / grid**3)
+
+
+def columns_kernel(
+    columns,
+    small_ref,
+    form_ref,
+    far_ref,
+    table_ref,
+    pot_ref,
+    got_ref,
+    send_ref,
+    fold_ref,
+    phase_ref,
+    sems,
+    first_ref,
+    second_ref,
+):
+    groups, _, rows = phase_ref.shape
+    atoms = phase_ref.shape[1] // 2
+    grid = table_ref.shape[1]
+    owners, planes, _ = send_ref.shape
+    channels = form_ref.shape[0]
+    step = pl.program_id(0)
+
+    @pl.when(step == 0)
+    def to_depth():
+        fetch(far_ref, phase_ref, sems)
+        ticks = lax.broadcasted_iota(jnp.int32, (columns, rows), 0)
+        deep = lax.broadcasted_iota(jnp.int32, (grid, rows), 0)
+        total = jnp.zeros((4 * columns, grid), f32)
+        for s in range(groups):
+            psi_re = two_rows(got_ref, s, 0)
+            psi_im = two_rows(got_ref, s, 2)
+            cell = small_ref[s : s + 1, :]
+            depth_hot = (deep == lax.div(cell, columns)).astype(f32).astype(bf16)
+            hot = ticks == lax.rem(cell, columns)
+            spread = jnp.concatenate(
+                [jnp.where(hot, psi_re, 0.0), jnp.where(hot, psi_im, 0.0)], 0
+            )
+            total = total + dot(jnp.concatenate(split(spread), 0), depth_hot, 1, 1)
+            form = form_ref[:, s, :]
+            weighted_re = (form * psi_re).astype(bf16)
+            weighted_im = (form * psi_im).astype(bf16)
+            first_ref[s] = jnp.concatenate([weighted_re, weighted_im], 0)
+            second_ref[s] = jnp.concatenate([-weighted_im, weighted_re], 0)
+        column = split(total[: 2 * columns] + total[2 * columns :])
+        by_cos = dot3((table_ref[0], table_ref[1]), column, 1, 1)
+        by_sin = dot3((table_ref[2], table_ref[3]), column, 1, 1)
+        deep_re = by_cos[:, :columns] - by_sin[:, columns:]
+        deep_im = by_sin[:, :columns] + by_cos[:, columns:]
+        for k in range(planes):
+            lines = slice(owners * k, owners * (k + 1))
+            send_ref[:, k, 0 : 2 * columns] = jnp.concatenate([deep_re[lines], deep_im[lines]], 1)
+        fold(pot_ref, fold_ref)
+
+    @pl.when(step == 1)
+    def to_products():
+        products = jnp.zeros((atoms, 2 * channels), f32)
+        copies = make_copies(far_ref, phase_ref, sems)
+        for s in range(groups):
+            copies[s].wait()
+            products = products + (
+                dot(phase_ref[s, 0:atoms, :], first_ref[s], 1, 1)
+                + dot(phase_ref[s, atoms : 2 * atoms, :], second_ref[s], 1, 1)
+            )
+        parts = [products[owners * k : owners * (k + 1)] for k in range(atoms // owners)]
+        half = len(parts) // 2
+        overlap = jnp.sum(got_ref[:, 4:8, :], 0).T
+        own = jnp.concatenate(
+            [overlap[:owners], overlap[owners:], jnp.zeros((owners, 2 * columns - 8), f32)], 1
+        )
+        extra = [jnp.concatenate(parts[:half], 1), jnp.concatenate(parts[half:], 1), own]
+        for k in range(planes):
+            send_ref[:, k, 2 * columns :] = extra[k]
 
 
 def planes_kernel(
@@ -533,7 +557,22 @@
         send_ref[s, 4:8, :] = overlap
 
 
-def products_kernel(waves, basis_ref, got_ref, image_ref, send_ref):
+def overlap(waves, got_ref, over_ref):
+    size = over_ref.shape[0] // 2
+    packed = jnp.concatenate([got_ref[d, 4:8, :] for d in range(got_ref.shape[0])], 0)
+    packed = unstripe(packed, 2) * (1.0 / waves)
+    line = lax.broadcasted_iota(jnp.int32, (size, size), 0)
+    spot = lax.broadcasted_iota(jnp.int32, (size, size), 1)
+    turned = packed.T
+    over_re = jnp.where(line <= spot, packed, turned)
+    over_im = jnp.where(line < spot, -turned, jnp.where(line > spot, packed, 0.0))
+    over_ref[...] = jnp.concatenate(
+        [jnp.concatenate([over_re, -over_im], 1), jnp.concatenate([over_im, over_re], 1)], 0
+    )
+
+
+def products_kernel(waves, basis_ref, got_ref, image_ref, over_ref, send_ref):
+    overlap(waves, got_ref, over_ref)
     bands = got_ref.shape[0]
     half = basis_ref.shape[0] // 2
     owners = send_ref.shape[0]
@@ -555,20 +594,6 @@
         [stripes(coef, bands), stripes(packed, bands), jnp.zeros((1, 128 - bands * bands), f32)], 1
     )
     send_ref[:, 0, :] = jnp.broadcast_to(row, (owners, row.shape[1]))
-
-
-def overlap_kernel(waves, got_ref, over_ref):
-    size = over_ref.shape[0] // 2
-    packed = jnp.concatenate([got_ref[d, 4:8, :] for d in range(got_ref.shape[0])], 0)
-    packed = unstripe(packed, 2) * (1.0 / waves)
-    line = lax.broadcasted_iota(jnp.int32, (size, size), 0)
-    spot = lax.broadcasted_iota(jnp.int32, (size, size), 1)
-    turned = packed.T
-    over_re = jnp.where(line <= spot, packed, turned)
-    over_im = jnp.where(line < spot, -turned, jnp.where(line > spot, packed, 0.0))
-    over_ref[...] = jnp.concatenate(
-        [jnp.concatenate([over_re, -over_im], 1), jnp.concatenate([over_im, over_re], 1)], 0
-    )
 
 
 def gather_kernel(got_ref, send_ref):
@@ -710,19 +735,21 @@
         vmem=8,
         flops=10**7,
     )
-    send = kernel_call(
+    send, folded = kernel_call(
         lambda *refs: columns_kernel(columns, *refs),
-        shape(owners, planes, 128),
+        (shape(owners, planes, 128), shape(planes, 2 * half_x, 2 * half_y)),
         small,
         form_factors,
         far_phase,
         owner_table,
+        potential,
         psi,
-        scratch=phase_scratch,
+        scratch=phase_scratch
+        + (pltpu.VMEM((band_count, 16, row_count), bf16),) * 2,
         far=(2,),
+        grid=(2,),
     )
     got = exchange(send, "pw")
-    folded = kernel_call(fold_kernel, shape(planes, 2 * half_x, 2 * half_y), potential)
     send, phase = kernel_call(
         lambda *refs: planes_kernel(columns, grid, *refs),
         (shape(owners, planes, 128), shape(*phase_dims, dtype=bf16)),
@@ -757,14 +784,15 @@
         got,
     )
     got = exchange(send, "band")
-    image, send = kernel_call(
+    image, over, send = kernel_call(
         lambda *refs: products_kernel(waves, *refs),
-        (shape(2 * slab, row_count), shape(len(near[0]), 1, 9 * 128)),
+        (
+            shape(2 * slab, row_count),
+            shape(2 * rows, 2 * rows),
+            shape(len(near[0]), 1, 9 * 128),
+        ),
         basis,
         got,
-    )
-    over = kernel_call(
-        lambda *refs: overlap_kernel(waves, *refs), shape(2 * rows, 2 * rows), got
     )
     got = exchange(send, ("band", "pw"), near)
     send = kernel_call(gather_kernel, shape(len(far[0]), 1, 9 * 128), got)

time: 117 us -> 116 us (level)
  blocking collectives: 38.9 us -> 76.1 us
  waiting for transfers between devices: 21.7 us -> 0.99 us
  starting transfers between devices: 26.6 us -> 10.9 us
  Pallas kernels: 28.2 us -> 25.7 us
    all_to_all x3 -> x5, blocking collectives: 38.9 us -> 76.1 us  [exchange(): lax.all_to_all(part, axis, split_axis=0, concat_axis=0, axis_index_groups...]
    all_to_all x3 -> x1, waiting for transfers between devices: 21.7 us -> 0.99 us  [exchange(): lax.all_to_all(part, axis, split_axis=0, concat_axis=0, axis_index_groups...]
    all_to_all x3 -> x1, starting transfers between devices: 26.6 us -> 10.9 us  [exchange(): lax.all_to_all(part, axis, split_axis=0, concat_axis=0, axis_index_groups...]
    pallas_call x10 -> x8, Pallas kernels: 28.2 us -> 25.7 us  [kernel_call(): pl.pallas_call(kernel, out_shape=outs, in_specs=[place[i in far] for i in...]
  transfers between devices with their start and end apart: 3 -> 1, of which waited for: 3 -> 1; matrix products, arithmetic and copies ran while one was open for 0% -> 0% of each run, Pallas kernels for 6% -> 4%
where the time goes in v3:
time: 116 us; the launch traced here: 115 us
  blocking collectives  76.1 us (66%)
  Pallas kernels  25.7 us (22%)
  starting transfers between devices  10.9 us (9%)
    all_to_all x5, blocking collectives, exchange(): lax.all_to_all(part, axis, split_axis=0, concat_axis=0, axis_index_groups...  76.1 us
    pallas_call x8, Pallas kernels, kernel_call(): pl.pallas_call(kernel, out_shape=outs, in_specs=[place[i in far] for i in...  25.7 us
    all_to_all x1, starting transfers between devices, exchange(): lax.all_to_all(part, axis, split_axis=0, concat_axis=0, axis_index_groups...  10.9 us
  transfers between devices with their start and end apart: 1, of which 1 were waited for; matrix products, arithmetic and copies ran while one was open for 0% of the time, Pallas kernels for 4%

profile of v3, /device:TPU:1, one launch (start us, length us, event | category | flops | bytes accessed | tf_op | source)
XLA Modules:
  0.0 115.2 jit_solution(14475952391238363301)
XLA Ops:
  0.6 0.0 copy-start
  0.6 0.0 copy-start.1
  0.7 2.1 %shard_map.163 = (f32[128,256]{1,0:T(8,128)}, f32[8,8,128]{2,1,0:T(8,128)}, s32[24,256]{1,0:T(8,128)}) custom-call(f32[128,128]{1,0:T(8,128)} %bitcast.9, f32[128,128]{1,0:T(8,128)} %bitcast.10, s32[8,256]{1,0:T(8,128)} %far_map_ref.1, s32[16,128]{1,0:T(8,128)} %bitcast.11, s32[3,512]{1,0:T(4,128)} %far_sites_ref.1), custom_call_target="tpu_custom_call" | custom-call | flops 1000000 | bytes 4000000 | tf_op jit(solution)/shard_map/pallas_call | solution.py:96
  2.8 10.9 %all-to-all-start = ((f32[8,8,128]{2,1,0:T(8,128)}), f32[8,8,128]{2,1,0:T(8,128)S(1)}, u32[]{:S(2)}, u32[]{:S(2)}) async-start(f32[8,8,128]{2,1,0:T(8,128)} %get-tuple-element.24), calls=%async_computation | async-start | bytes 65536 | tf_op jit(solution)/shard_map/all_to_all | solution.py:687
  13.7 0.0 copy-start.3
  13.7 0.7 copy-done.3
  14.4 0.0 copy-start.4
  14.4 5.1 %shard_map.164.refs_2_.refs_4_ = bf16[128,1024,256]{2,1,0:T(8,128)(2,1)} custom-call(s32[24,256]{1,0:T(8,128)S(1)} %copy-done.3), custom_call_target="tpu_custom_call" | custom-call | flops 10000000 | bytes 4000000 | tf_op jit(solution)/shard_map/pallas_call | solution.py:96
  19.5 0.0 copy-start.8
  19.5 0.0 copy-start.9
  19.5 0.0 copy-start.2
  19.5 1.0 all-to-all-done.refs_5_.refs_6_
  20.5 0.0 copy-done
  20.5 0.0 copy-done.1
  20.5 0.0 copy-done.4
  20.5 0.0 copy-done.7
  20.6 4.8 %shard_map.165 = (f32[64,3,128]{2,1,0:T(4,128)S(1)}, f32[3,208,256]{2,1,0:T(8,128)S(1)}) custom-call(s32[24,256]{1,0:T(8,128)S(1)} %copy-done.4, f32[8,8,256]{2,1,0:T(8,128)S(1)} %copy-done.7, bf16[128,1024,256]{2,1,0:T(8,128)(2,1)} %shard_map.164.refs_2_.refs_4_, bf16[4,192,192]{2,1,0:T(8,128)(2,1)S(1)} %copy-done, f32[3,192,192]{2,1,0:T(8,128)S(1)} %copy-done.1, ...), custom_call_target="tpu_custom_call" | custom-call | flops 1000000 | bytes 4000000 | tf_op jit(solution)/shard_map/pallas_call | solution.py:96
  25.3 23.1 %all_to_all.30.refs_5_ = f32[64,3,128]{2,1,0:T(4,128)S(1)} all-to-all(f32[64,3,128]{2,1,0:T(4,128)S(1)} %get-tuple-element.26), channel_id=1, replica_groups=mesh['band'=8,'pw'=64] {'pw'}, dimensions={0} | all-to-all | bytes 196608 | tf_op jit(solution)/shard_map/all_to_all | solution.py:687
  48.5 0.0 copy-done.5
  48.5 0.0 copy-done.6
  48.5 10.0 %shard_map.166 = (f32[64,3,128]{2,1,0:T(4,128)S(1)}, bf16[8,1024,256]{2,1,0:T(8,128)(2,1)S(1)}) custom-call(s32[24,256]{1,0:T(8,128)S(1)} %copy-done.4, f32[3,208,256]{2,1,0:T(8,128)S(1)} %get-tuple-element.25.refs_1_, bf16[208,624]{1,0:T(8,128)(2,1)S(1)} %copy-done.6, bf16[768,256]{1,0:T(8,128)(2,1)S(1)} %copy-done.5, ...), custom_call_target="tpu_custom_call" | custom-call | flops 1000000 | bytes 4000000 | tf_op jit(solution)/shard_map/pallas_call | solution.py:96
  58.5 14.9 %all_to_all.31.refs_7_ = f32[64,3,128]{2,1,0:T(4,128)S(1)} all-to-all(f32[64,3,128]{2,1,0:T(4,128)S(1)} %get-tuple-element.28), channel_id=1, replica_groups=mesh['band'=8,'pw'=64] {'pw'}, dimensions={0} | all-to-all | bytes 196608 | tf_op jit(solution)/shard_map/all_to_all | solution.py:687
  73.4 0.0 copy-done.8
  73.4 0.0 copy-done.9
  73.4 1.2 %shard_map.167 = f32[8,8,128]{2,1,0:T(8,128)S(1)} custom-call(s32[24,256]{1,0:T(8,128)S(1)} %copy-done.4, f32[8,8,256]{2,1,0:T(8,128)S(1)} %copy-done.7, f32[8,256]{1,0:T(8,128)S(1)} %copy-done.8, f32[1,8]{1,0:T(1,128)S(1)} %bitcast.8, bf16[8,1024,256]{2,1,0:T(8,128)(2,1)S(1)} %get-tuple-element.27.refs_4_, bf16[4,192,192]{2,1,0:T(8,128)(2,1)S(1)} %copy-done, ...), custom_call_target="tpu_custom_call" | custom-call | flops 1000000 | bytes 4000000 | tf_op jit(solution)/shard_map/pallas_call | solution.py:96
  74.6 11.6 %all_to_all.32.refs_1_ = f32[8,8,128]{2,1,0:T(8,128)S(1)} all-to-all(f32[8,8,128]{2,1,0:T(8,128)S(1)} %shard_map.167), channel_id=1, replica_groups=mesh['band'=8,'pw'=64] {'band'}, dimensions={0} | all-to-all | bytes 65536 | tf_op jit(solution)/shard_map/all_to_all | solution.py:687
  86.2 0.0 copy-done.2
  86.2 0.5 shard_map.168
  86.8 11.9 %all_to_all.33.got_ref = f32[32,1,1152]{2,1,0:T(1,128)S(1)} all-to-all(f32[32,1,1152]{2,1,0:T(1,128)S(1)} %get-tuple-element.31), channel_id=1, replica_groups={{0,1,2,3,4,5,6,7,8,9,10,11,12,13,14,15,64,65,66,67,68,69,70,71,72,73,74..., dimensions={0} | all-to-all | bytes 294912 | tf_op jit(solution)/shard_map/all_to_all | solution.py:687
  98.6 0.1 shard_map.169
  98.7 14.5 %all_to_all.34.got_ref = f32[16,1,1152]{2,1,0:T(1,128)S(1)} all-to-all(f32[16,1,1152]{2,1,0:T(1,128)S(1)} %shard_map.169), channel_id=1, replica_groups={{0,16,32,48,128,144,160,176,256,272,288,304,384,400,416,432},{1,17,33,4..., dimensions={0} | all-to-all | bytes 147456 | tf_op jit(solution)/shard_map/all_to_all | solution.py:687
  113.2 1.9 %shard_map.170 = (f32[16,128]{1,0:T(8,128)}, f32[16,128]{1,0:T(8,128)}, f32[64,8]{1,0:T(8,128)}, f32[64,8]{1,0:T(8,128)}, f32[8,8]{1,0:T(8,128)}, /*index=5*/f32[8,8]{1,0:T(8,128)}) custom-call(f32[128,256]{1,0:T(8,128)S(1)} %copy-done.2, f32[16,256]{1,0:T(8,128)S(1)} %get-tuple-element.29.image_ref, f32[128,128]{1,0:T(8,128)S(1)} %get-tuple-element.30.over_ref, ...), custom_call_target="tpu_custom_call" | custom-call | flops 1000000 | bytes 4000000 | tf_op jit(solution)/shard_map/pallas_call | solution.py:96
  (3 shorter events, 0.0 us)
Async XLA Ops:
  0.6 19.9 %copy-start = (bf16[4,192,192]{2,1,0:T(8,128)(2,1)S(1)}, bf16[4,192,192]{2,1,0:T(8,128)(2,1)}, u32[]{:S(2)}) copy-start(bf16[4,192,192]{2,1,0:T(8,128)(2,1)} %constant.6.clone.refs_3_.refs_5_) | copy-start | bytes 884740
  0.6 19.9 %copy-start.1 = (f32[3,192,192]{2,1,0:T(8,128)S(1)}, f32[3,192,192]{2,1,0:T(8,128)}, u32[]{:S(2)}) copy-start(f32[3,192,192]{2,1,0:T(8,128)} %refs_4_.1) | copy-start | bytes 1327108
  2.8 17.8 %all-to-all-start = ((f32[8,8,128]{2,1,0:T(8,128)}), f32[8,8,128]{2,1,0:T(8,128)S(1)}, u32[]{:S(2)}, u32[]{:S(2)}) async-start(f32[8,8,128]{2,1,0:T(8,128)} %get-tuple-element.24), calls=%async_computation | async-start | bytes 65536 | tf_op jit(solution)/shard_map/all_to_all | solution.py:687
  13.7 0.7 copy-start.3
  14.4 6.1 %copy-start.4 = (s32[24,256]{1,0:T(8,128)S(1)}, s32[24,256]{1,0:T(8,128)}, u32[]{:S(2)}) copy-start(s32[24,256]{1,0:T(8,128)} %get-tuple-element.23.refs_0_) | copy-start | bytes 73732
  14.4 6.2 %copy-start.7 = (f32[8,8,256]{2,1,0:T(8,128)S(1)}, f32[8,8,256]{2,1,0:T(8,128)}, u32[]{:S(2)}) copy-start(f32[8,8,256]{2,1,0:T(8,128)} %refs_1_.3) | copy-start | bytes 196612
  14.4 34.1 %copy-start.5 = (bf16[768,256]{1,0:T(8,128)(2,1)S(1)}, bf16[768,256]{1,0:T(8,128)(2,1)}, u32[]{:S(2)}) copy-start(bf16[768,256]{1,0:T(8,128)(2,1)} %constant.8.clone.refs_3_) | copy-start | bytes 1179652
  14.4 34.1 %copy-start.6 = (bf16[208,624]{1,0:T(8,128)(2,1)S(1)}, bf16[208,624]{1,0:T(8,128)(2,1)}, u32[]{:S(2)}) copy-start(bf16[208,624]{1,0:T(8,128)(2,1)} %constant.7.clone.refs_2_) | copy-start | bytes 778756
  19.5 53.9 %copy-start.8 = (f32[8,256]{1,0:T(8,128)S(1)}, f32[8,256]{1,0:T(8,128)}, u32[]{:S(2)}) copy-start(f32[8,256]{1,0:T(8,128)} %refs_2_.2) | copy-start | bytes 24580
  19.5 53.9 %copy-start.9 = (f32[8]{0:T(128)S(1)}, f32[8]{0:T(128)}, u32[]{:S(2)}) copy-start(f32[8]{0:T(128)} %param.17) | copy-start | bytes 100
  19.5 66.7 %copy-start.2 = (f32[128,256]{1,0:T(8,128)S(1)}, f32[128,256]{1,0:T(8,128)}, u32[]{:S(2)}) copy-start(f32[128,256]{1,0:T(8,128)} %get-tuple-element.22.refs_0_.basis_ref) | copy-start | bytes 393220

commit v4 on v3

--- a/solution.py
+++ b/solution.py
@@ -100,7 +100,7 @@
         scratch_shapes=scratch,
         grid=grid,
         out_specs=tuple(place[i in far_out] for i in range(len(outs))),
-        compiler_params=pltpu.CompilerParams(vmem_limit_bytes=vmem * 2**20),
+        compiler_params=pltpu.CompilerParams(vmem_limit_bytes=int(vmem * 2**20)),
         cost_estimate=pl.CostEstimate(flops=flops, bytes_accessed=4 * 10**6, transcendentals=0),
     )(*args)
     return out[0] if single else out
@@ -320,14 +320,17 @@
         for k in range(planes):
             lines = slice(owners * k, owners * (k + 1))
             send_ref[:, k, 0 : 2 * columns] = jnp.concatenate([deep_re[lines], deep_im[lines]], 1)
+
+    @pl.when(step == 1)
+    def space():
         fold(pot_ref, fold_ref)
 
-    @pl.when(step == 1)
+    @pl.when(step == 2)
     def to_products():
         products = jnp.zeros((atoms, 2 * channels), f32)
-        copies = make_copies(far_ref, phase_ref, sems)
+        for copy in make_copies(far_ref, phase_ref, sems):
+            copy.wait()
         for s in range(groups):
-            copies[s].wait()
             products = products + (
                 dot(phase_ref[s, 0:atoms, :], first_ref[s], 1, 1)
                 + dot(phase_ref[s, atoms : 2 * atoms, :], second_ref[s], 1, 1)
@@ -692,8 +695,8 @@
     for z in range(band_count):
         for p in range(owners):
             y, rest = divmod(p, 8)
-            near.setdefault((z // 2, y // 2), []).append(z * owners + p)
-            far.setdefault((z % 2, y % 2, rest), []).append(z * owners + p)
+            near.setdefault((z // 2, y), []).append(z * owners + p)
+            far.setdefault((z % 2, rest), []).append(z * owners + p)
     near, far = list(near.values()), list(far.values())
 
     places = column_map.reshape(-1, 128)
@@ -747,7 +750,7 @@
         scratch=phase_scratch
         + (pltpu.VMEM((band_count, 16, row_count), bf16),) * 2,
         far=(2,),
-        grid=(2,),
+        grid=(3,),
     )
     got = exchange(send, "pw")
     send, phase = kernel_call(

time: 116 us -> 114 us (0.983)
  blocking collectives: 76.1 us -> 74.4 us
    all_to_all x5, blocking collectives: 76.1 us -> 74.4 us  [exchange(): lax.all_to_all(part, axis, split_axis=0, concat_axis=0, axis_index_groups...]
  transfers between devices with their start and end apart: 1 -> 1, of which waited for: 1 -> 1; matrix products, arithmetic and copies ran while one was open for 0% -> 0% of each run, Pallas kernels for 4% -> 5%
where the time goes in v4:
time: 114 us; the launch traced here: 113 us
  blocking collectives  74.4 us (65%)
  Pallas kernels  25.4 us (22%)
  starting transfers between devices  10.9 us (10%)
    all_to_all x5, blocking collectives, exchange(): lax.all_to_all(part, axis, split_axis=0, concat_axis=0, axis_index_groups...  74.4 us
    pallas_call x8, Pallas kernels, kernel_call(): pl.pallas_call(kernel, out_shape=outs, in_specs=[place[i in far] for i in...  25.4 us
    all_to_all x1, starting transfers between devices, exchange(): lax.all_to_all(part, axis, split_axis=0, concat_axis=0, axis_index_groups...  10.9 us
  transfers between devices with their start and end apart: 1, of which 1 were waited for; matrix products, arithmetic and copies ran while one was open for 0% of the time, Pallas kernels for 5%

profile of v4, /device:TPU:1, one launch (start us, length us, event | category | flops | bytes accessed | tf_op | source)
XLA Modules:
  0.0 113.2 jit_solution(6162193442088297147)
XLA Ops:
  0.6 0.0 copy-start
  0.6 0.0 copy-start.1
  0.7 2.1 %shard_map.163 = (f32[128,256]{1,0:T(8,128)}, f32[8,8,128]{2,1,0:T(8,128)}, s32[24,256]{1,0:T(8,128)}) custom-call(f32[128,128]{1,0:T(8,128)} %bitcast.9, f32[128,128]{1,0:T(8,128)} %bitcast.10, s32[8,256]{1,0:T(8,128)} %far_map_ref.1, s32[16,128]{1,0:T(8,128)} %bitcast.11, s32[3,512]{1,0:T(4,128)} %far_sites_ref.1), custom_call_target="tpu_custom_call" | custom-call | flops 1000000 | bytes 4000000 | tf_op jit(solution)/shard_map/pallas_call | solution.py:96
  2.8 10.9 %all-to-all-start = ((f32[8,8,128]{2,1,0:T(8,128)}), f32[8,8,128]{2,1,0:T(8,128)S(1)}, u32[]{:S(2)}, u32[]{:S(2)}) async-start(f32[8,8,128]{2,1,0:T(8,128)} %get-tuple-element.24), calls=%async_computation | async-start | bytes 65536 | tf_op jit(solution)/shard_map/all_to_all | solution.py:690
  13.7 0.0 copy-start.3
  13.7 0.7 copy-done.3
  14.4 0.0 copy-start.4
  14.4 0.0 copy-start.7
  14.4 5.1 %shard_map.164.refs_2_.refs_4_ = bf16[128,1024,256]{2,1,0:T(8,128)(2,1)} custom-call(s32[24,256]{1,0:T(8,128)S(1)} %copy-done.3), custom_call_target="tpu_custom_call" | custom-call | flops 10000000 | bytes 4000000 | tf_op jit(solution)/shard_map/pallas_call | solution.py:96
  19.5 0.0 copy-start.8
  19.5 0.0 copy-start.9
  19.5 0.0 copy-start.2
  19.5 1.0 all-to-all-done.refs_5_.refs_6_
  20.5 0.0 copy-done
  20.5 0.0 copy-done.1
  20.5 0.0 copy-done.4
  20.5 0.0 copy-done.7
  20.6 4.5 %shard_map.165 = (f32[64,3,128]{2,1,0:T(4,128)S(1)}, f32[3,208,256]{2,1,0:T(8,128)S(1)}) custom-call(s32[24,256]{1,0:T(8,128)S(1)} %copy-done.4, f32[8,8,256]{2,1,0:T(8,128)S(1)} %copy-done.7, bf16[128,1024,256]{2,1,0:T(8,128)(2,1)} %shard_map.164.refs_2_.refs_4_, bf16[4,192,192]{2,1,0:T(8,128)(2,1)S(1)} %copy-done, f32[3,192,192]{2,1,0:T(8,128)S(1)} %copy-done.1, ...), custom_call_target="tpu_custom_call" | custom-call | flops 1000000 | bytes 4000000 | tf_op jit(solution)/shard_map/pallas_call | solution.py:96
  25.0 23.1 %all_to_all.30.refs_5_ = f32[64,3,128]{2,1,0:T(4,128)S(1)} all-to-all(f32[64,3,128]{2,1,0:T(4,128)S(1)} %get-tuple-element.26), channel_id=1, replica_groups=mesh['band'=8,'pw'=64] {'pw'}, dimensions={0} | all-to-all | bytes 196608 | tf_op jit(solution)/shard_map/all_to_all | solution.py:690
  48.2 0.0 copy-done.5
  48.2 0.0 copy-done.6
  48.2 10.0 %shard_map.166 = (f32[64,3,128]{2,1,0:T(4,128)S(1)}, bf16[8,1024,256]{2,1,0:T(8,128)(2,1)S(1)}) custom-call(s32[24,256]{1,0:T(8,128)S(1)} %copy-done.4, f32[3,208,256]{2,1,0:T(8,128)S(1)} %get-tuple-element.25.refs_1_, bf16[208,624]{1,0:T(8,128)(2,1)S(1)} %copy-done.6, bf16[768,256]{1,0:T(8,128)(2,1)S(1)} %copy-done.5, ...), custom_call_target="tpu_custom_call" | custom-call | flops 1000000 | bytes 4000000 | tf_op jit(solution)/shard_map/pallas_call | solution.py:96
  58.2 14.9 %all_to_all.31.refs_7_ = f32[64,3,128]{2,1,0:T(4,128)S(1)} all-to-all(f32[64,3,128]{2,1,0:T(4,128)S(1)} %get-tuple-element.28), channel_id=1, replica_groups=mesh['band'=8,'pw'=64] {'pw'}, dimensions={0} | all-to-all | bytes 196608 | tf_op jit(solution)/shard_map/all_to_all | solution.py:690
  73.1 0.0 copy-done.8
  73.1 0.0 copy-done.9
  73.1 1.2 %shard_map.167 = f32[8,8,128]{2,1,0:T(8,128)S(1)} custom-call(s32[24,256]{1,0:T(8,128)S(1)} %copy-done.4, f32[8,8,256]{2,1,0:T(8,128)S(1)} %copy-done.7, f32[8,256]{1,0:T(8,128)S(1)} %copy-done.8, f32[1,8]{1,0:T(1,128)S(1)} %bitcast.8, bf16[8,1024,256]{2,1,0:T(8,128)(2,1)S(1)} %get-tuple-element.27.refs_4_, bf16[4,192,192]{2,1,0:T(8,128)(2,1)S(1)} %copy-done, ...), custom_call_target="tpu_custom_call" | custom-call | flops 1000000 | bytes 4000000 | tf_op jit(solution)/shard_map/pallas_call | solution.py:96
  74.4 11.6 %all_to_all.32.refs_1_ = f32[8,8,128]{2,1,0:T(8,128)S(1)} all-to-all(f32[8,8,128]{2,1,0:T(8,128)S(1)} %shard_map.167), channel_id=1, replica_groups=mesh['band'=8,'pw'=64] {'band'}, dimensions={0} | all-to-all | bytes 65536 | tf_op jit(solution)/shard_map/all_to_all | solution.py:690
  86.0 0.0 copy-done.2
  86.0 0.5 shard_map.168
  86.5 10.1 %all_to_all.33.got_ref = f32[16,1,1152]{2,1,0:T(1,128)S(1)} all-to-all(f32[16,1,1152]{2,1,0:T(1,128)S(1)} %get-tuple-element.31), channel_id=1, replica_groups={{0,1,2,3,4,5,6,7,64,65,66,67,68,69,70,71},{8,9,10,11,12,13,14,15,72,73,..., dimensions={0} | all-to-all | bytes 147456 | tf_op jit(solution)/shard_map/all_to_all | solution.py:690
  96.7 14.6 %all_to_all.34.got_ref = f32[32,1,1152]{2,1,0:T(1,128)S(1)} all-to-all(f32[32,1,1152]{2,1,0:T(1,128)S(1)} %shard_map.169), channel_id=1, replica_groups={{0,8,16,24,32,40,48,56,128,136,144,152,160,168,176,184,256,264,272,280,..., dimensions={0} | all-to-all | bytes 294912 | tf_op jit(solution)/shard_map/all_to_all | solution.py:690
  111.3 1.9 %shard_map.170 = (f32[16,128]{1,0:T(8,128)}, f32[16,128]{1,0:T(8,128)}, f32[64,8]{1,0:T(8,128)}, f32[64,8]{1,0:T(8,128)}, f32[8,8]{1,0:T(8,128)}, /*index=5*/f32[8,8]{1,0:T(8,128)}) custom-call(f32[128,256]{1,0:T(8,128)S(1)} %copy-done.2, f32[16,256]{1,0:T(8,128)S(1)} %get-tuple-element.29.image_ref, f32[128,128]{1,0:T(8,128)S(1)} %get-tuple-element.30.over_ref, ...), custom_call_target="tpu_custom_call" | custom-call | flops 1000000 | bytes 4000000 | tf_op jit(solution)/shard_map/pallas_call | solution.py:96
  (3 shorter events, 0.0 us)
Async XLA Ops:
  0.6 19.9 %copy-start = (bf16[4,192,192]{2,1,0:T(8,128)(2,1)S(1)}, bf16[4,192,192]{2,1,0:T(8,128)(2,1)}, u32[]{:S(2)}) copy-start(bf16[4,192,192]{2,1,0:T(8,128)(2,1)} %constant.6.clone.refs_3_.refs_5_) | copy-start | bytes 884740
  0.6 19.9 %copy-start.1 = (f32[3,192,192]{2,1,0:T(8,128)S(1)}, f32[3,192,192]{2,1,0:T(8,128)}, u32[]{:S(2)}) copy-start(f32[3,192,192]{2,1,0:T(8,128)} %refs_4_.1) | copy-start | bytes 1327108
  2.8 17.8 %all-to-all-start = ((f32[8,8,128]{2,1,0:T(8,128)}), f32[8,8,128]{2,1,0:T(8,128)S(1)}, u32[]{:S(2)}, u32[]{:S(2)}) async-start(f32[8,8,128]{2,1,0:T(8,128)} %get-tuple-element.24), calls=%async_computation | async-start | bytes 65536 | tf_op jit(solution)/shard_map/all_to_all | solution.py:690
  13.7 0.7 copy-start.3
  14.4 6.1 %copy-start.4 = (s32[24,256]{1,0:T(8,128)S(1)}, s32[24,256]{1,0:T(8,128)}, u32[]{:S(2)}) copy-start(s32[24,256]{1,0:T(8,128)} %get-tuple-element.23.refs_0_) | copy-start | bytes 73732
  14.4 6.2 %copy-start.7 = (f32[8,8,256]{2,1,0:T(8,128)S(1)}, f32[8,8,256]{2,1,0:T(8,128)}, u32[]{:S(2)}) copy-start(f32[8,8,256]{2,1,0:T(8,128)} %refs_1_.3) | copy-start | bytes 196612
  14.4 33.8 %copy-start.5 = (bf16[768,256]{1,0:T(8,128)(2,1)S(1)}, bf16[768,256]{1,0:T(8,128)(2,1)}, u32[]{:S(2)}) copy-start(bf16[768,256]{1,0:T(8,128)(2,1)} %constant.8.clone.refs_3_) | copy-start | bytes 1179652
  14.4 33.8 %copy-start.6 = (bf16[208,624]{1,0:T(8,128)(2,1)S(1)}, bf16[208,624]{1,0:T(8,128)(2,1)}, u32[]{:S(2)}) copy-start(bf16[208,624]{1,0:T(8,128)(2,1)} %constant.7.clone.refs_2_) | copy-start | bytes 778756
  19.5 53.6 %copy-start.8 = (f32[8,256]{1,0:T(8,128)S(1)}, f32[8,256]{1,0:T(8,128)}, u32[]{:S(2)}) copy-start(f32[8,256]{1,0:T(8,128)} %refs_2_.2) | copy-start | bytes 24580
  19.5 53.6 %copy-start.9 = (f32[8]{0:T(128)S(1)}, f32[8]{0:T(128)}, u32[]{:S(2)}) copy-start(f32[8]{0:T(128)} %param.17) | copy-start | bytes 100
  19.5 66.4 %copy-start.2 = (f32[128,256]{1,0:T(8,128)S(1)}, f32[128,256]{1,0:T(8,128)}, u32[]{:S(2)}) copy-start(f32[128,256]{1,0:T(8,128)} %get-tuple-element.22.refs_0_.basis_ref) | copy-start | bytes 393220

commit v5 on v4

--- a/solution.py
+++ b/solution.py
@@ -89,7 +89,7 @@
     return jnp.concatenate([part[:, i * width : (i + 1) * width] for i in range(count)], 0)
 
 
-def kernel_call(kernel, outs, *args, flops=10**6, vmem=8, scratch=(), far=(), far_out=(), grid=()):
+def kernel_call(kernel, outs, *args, flops=10**6, vmem=8, scratch=(), far=(), far_out=(), grid=(), aliases=None):
     single = not isinstance(outs, tuple)
     outs = (outs,) if single else outs
     place = (pl.BlockSpec(memory_space=pltpu.VMEM), pl.BlockSpec(memory_space=pltpu.HBM))
@@ -99,6 +99,7 @@
         in_specs=[place[i in far] for i in range(len(args))],
         scratch_shapes=scratch,
         grid=grid,
+        input_output_aliases=aliases or {},
         out_specs=tuple(place[i in far_out] for i in range(len(outs))),
         compiler_params=pltpu.CompilerParams(vmem_limit_bytes=int(vmem * 2**20)),
         cost_estimate=pl.CostEstimate(flops=flops, bytes_accessed=4 * 10**6, transcendentals=0),
@@ -183,12 +184,9 @@
         send_ref[band, 4:8, :] = packed[4 * band : 4 * band + 4, :]
 
 
-def phase_kernel(grid, columns, small_ref, far_ref, phase_ref, sems):
+def phase_blocks(grid, columns, small_ref, phase_ref, blocks):
     groups, _, rows = phase_ref.shape
     atoms = phase_ref.shape[1] // 2
-    copies = [
-        pltpu.make_async_copy(phase_ref.at[s], far_ref.at[s], sems.at[s]) for s in range(groups)
-    ]
     root = math.sqrt(2.0)
     cos_poly = [root * c / grid ** (2 * k) for k, c in enumerate(COS_POLY)]
     sin_poly = [root * c / grid ** (2 * k + 1) for k, c in enumerate(SIN_POLY)]
@@ -207,7 +205,7 @@
     column_x = lax.div(mine, grid).astype(f32)
     column_y = lax.rem(mine, grid).astype(f32)
     ticks = lax.broadcasted_iota(jnp.int32, (columns, rows), 0)
-    for s in range(groups):
+    for s in blocks:
         cell = small_ref[s : s + 1, :]
         depth = lax.div(cell, columns).astype(f32)
         hot = ticks == lax.rem(cell, columns)
@@ -226,6 +224,14 @@
         h = h * turns
         phase_ref[s, 0:atoms, :] = (1.0 - h * h).astype(bf16)
         phase_ref[s, atoms : 2 * atoms, :] = (h * c).astype(bf16)
+        yield s
+
+
+def phase_kernel(grid, columns, first, small_ref, far_ref, phase_ref, sems):
+    copies = [
+        pltpu.make_async_copy(phase_ref.at[s], far_ref.at[s], sems.at[s]) for s in range(first)
+    ]
+    for s in phase_blocks(grid, columns, small_ref, phase_ref, range(first)):
         copies[s].start()
     for copy in copies:
         copy.wait()
@@ -271,14 +277,16 @@
 
 def columns_kernel(
     columns,
+    first,
     small_ref,
     form_ref,
-    far_ref,
+    _,
     table_ref,
     pot_ref,
     got_ref,
     send_ref,
     fold_ref,
+    far_ref,
     phase_ref,
     sems,
     first_ref,
@@ -290,10 +298,15 @@
     owners, planes, _ = send_ref.shape
     channels = form_ref.shape[0]
     step = pl.program_id(0)
+    copies = []
+    for s in range(groups):
+        ends = (far_ref.at[s], phase_ref.at[s])
+        copies.append(pltpu.make_async_copy(*(ends if s < first else ends[::-1]), sems.at[s]))
 
     @pl.when(step == 0)
     def to_depth():
-        fetch(far_ref, phase_ref, sems)
+        for copy in copies[:first]:
+            copy.start()
         ticks = lax.broadcasted_iota(jnp.int32, (columns, rows), 0)
         deep = lax.broadcasted_iota(jnp.int32, (grid, rows), 0)
         total = jnp.zeros((4 * columns, grid), f32)
@@ -324,11 +337,13 @@
     @pl.when(step == 1)
     def space():
         fold(pot_ref, fold_ref)
+        for s in phase_blocks(grid, columns, small_ref, phase_ref, range(first, groups)):
+            copies[s].start()
 
     @pl.when(step == 2)
     def to_products():
         products = jnp.zeros((atoms, 2 * channels), f32)
-        for copy in make_copies(far_ref, phase_ref, sems):
+        for copy in copies[:first]:
             copy.wait()
         for s in range(groups):
             products = products + (
@@ -344,6 +359,8 @@
         extra = [jnp.concatenate(parts[:half], 1), jnp.concatenate(parts[half:], 1), own]
         for k in range(planes):
             send_ref[:, k, 2 * columns :] = extra[k]
+        for copy in copies[first:]:
+            copy.wait()
 
 
 def planes_kernel(
@@ -727,10 +744,11 @@
     psi = exchange(send, "band")
 
     phase_dims = (band_count, 2 * atoms, row_count)
+    first = band_count - 2
     phase_sems = (pltpu.SemaphoreType.DMA((band_count,)),)
     phase_scratch = (pltpu.VMEM(phase_dims, bf16),) + phase_sems
     far_phase = kernel_call(
-        lambda *refs: phase_kernel(grid, columns, *refs),
+        lambda *refs: phase_kernel(grid, columns, first, *refs),
         shape(16 * band_count, *phase_dims[1:], dtype=bf16),
         small,
         scratch=phase_scratch,
@@ -738,9 +756,13 @@
         vmem=8,
         flops=10**7,
     )
-    send, folded = kernel_call(
-        lambda *refs: columns_kernel(columns, *refs),
-        (shape(owners, planes, 128), shape(planes, 2 * half_x, 2 * half_y)),
+    send, folded, far_phase = kernel_call(
+        lambda *refs: columns_kernel(columns, first, *refs),
+        (
+            shape(owners, planes, 128),
+            shape(planes, 2 * half_x, 2 * half_y),
+            shape(*far_phase.shape, dtype=bf16),
+        ),
         small,
         form_factors,
         far_phase,
@@ -750,6 +772,8 @@
         scratch=phase_scratch
         + (pltpu.VMEM((band_count, 16, row_count), bf16),) * 2,
         far=(2,),
+        far_out=(2,),
+        aliases={2: 2},
         grid=(3,),
     )
     got = exchange(send, "pw")

time: 114 us -> 113 us (level)
  Pallas kernels: 25.4 us -> 24.1 us
    pallas_call x8, Pallas kernels: 25.4 us -> 24.1 us  [kernel_call(): pl.pallas_call(kernel, out_shape=outs, in_specs=[place[i in far] for i in...]
  transfers between devices with their start and end apart: 1 -> 1, of which waited for: 1 -> 1; matrix products, arithmetic and copies ran while one was open for 0% -> 0% of each run, Pallas kernels for 5% -> 4%
where the time goes in v5:
time: 113 us; the launch traced here: 112 us
  blocking collectives  73.5 us (65%)
  Pallas kernels  24.1 us (21%)
  starting transfers between devices  10.9 us (10%)
  waiting for transfers between devices  1.94 us (2%)
    all_to_all x5, blocking collectives, exchange(): lax.all_to_all(part, axis, split_axis=0, concat_axis=0, axis_index_groups...  73.5 us
    pallas_call x8, Pallas kernels, kernel_call(): pl.pallas_call(kernel, out_shape=outs, in_specs=[place[i in far] for i in...  24.1 us
    all_to_all x1, starting transfers between devices, exchange(): lax.all_to_all(part, axis, split_axis=0, concat_axis=0, axis_index_groups...  10.9 us
  transfers between devices with their start and end apart: 1, of which 1 were waited for; matrix products, arithmetic and copies ran while one was open for 0% of the time, Pallas kernels for 4%

profile of v5, /device:TPU:1, one launch (start us, length us, event | category | flops | bytes accessed | tf_op | source)
XLA Modules:
  0.0 111.9 jit_solution(17318533787380789158)
XLA Ops:
  0.6 0.0 copy-start
  0.6 0.0 copy-start.1
  0.7 2.1 %shard_map.163 = (f32[128,256]{1,0:T(8,128)}, f32[8,8,128]{2,1,0:T(8,128)}, s32[24,256]{1,0:T(8,128)}) custom-call(f32[128,128]{1,0:T(8,128)} %bitcast.9, f32[128,128]{1,0:T(8,128)} %bitcast.10, s32[8,256]{1,0:T(8,128)} %far_map_ref.1, s32[16,128]{1,0:T(8,128)} %bitcast.11, s32[3,512]{1,0:T(4,128)} %far_sites_ref.1), custom_call_target="tpu_custom_call" | custom-call | flops 1000000 | bytes 4000000 | tf_op jit(solution)/shard_map/pallas_call | solution.py:96
  2.8 10.9 %all-to-all-start = ((f32[8,8,128]{2,1,0:T(8,128)}), f32[8,8,128]{2,1,0:T(8,128)S(1)}, u32[]{:S(2)}, u32[]{:S(2)}) async-start(f32[8,8,128]{2,1,0:T(8,128)} %get-tuple-element.25), calls=%async_computation | async-start | bytes 65536 | tf_op jit(solution)/shard_map/all_to_all | solution.py:707
  13.7 0.0 copy-start.3
  13.7 0.7 copy-done.3
  14.4 0.0 copy-start.4
  14.4 0.0 copy-start.7
  14.4 4.1 %shard_map.164.refs_2_ = bf16[128,1024,256]{2,1,0:T(8,128)(2,1)} custom-call(s32[24,256]{1,0:T(8,128)S(1)} %copy-done.3), custom_call_target="tpu_custom_call" | custom-call | flops 10000000 | bytes 4000000 | tf_op jit(solution)/shard_map/pallas_call | solution.py:96
  18.6 0.0 copy-start.8
  18.6 0.0 copy-start.9
  18.6 0.0 copy-start.2
  18.6 1.9 %all-to-all-done.refs_5_.refs_6_ = f32[8,8,128]{2,1,0:T(8,128)S(1)} async-done(((f32[8,8,128]{2,1,0:T(8,128)}), f32[8,8,128]{2,1,0:T(8,128)S(1)}, u32[]{:S(2)}, u32[]{:S(2)}) %all-to-all-start) | async-done | bytes 32800 | tf_op jit(solution)/shard_map/all_to_all | solution.py:707
  20.5 0.0 copy-done
  20.5 0.0 copy-done.1
  20.5 0.0 copy-done.4
  20.5 0.0 copy-done.7
  20.6 4.2 %shard_map.165 = (f32[64,3,128]{2,1,0:T(4,128)S(1)}, f32[3,208,256]{2,1,0:T(8,128)S(1)}, bf16[128,1024,256]{2,1,0:T(8,128)(2,1)}) custom-call(s32[24,256]{1,0:T(8,128)S(1)} %copy-done.4, f32[8,8,256]{2,1,0:T(8,128)S(1)} %copy-done.7, bf16[128,1024,256]{2,1,0:T(8,128)(2,1)} %shard_map.164.refs_2_, ...), custom_call_target="tpu_custom_call", output_to_operand_aliasing={{2}: (2, {})} | custom-call | flops 1000000 | bytes 4000000 | tf_op jit(solution)/shard_map/pallas_call | solution.py:96
  24.7 23.1 %all_to_all.30.refs_5_ = f32[64,3,128]{2,1,0:T(4,128)S(1)} all-to-all(f32[64,3,128]{2,1,0:T(4,128)S(1)} %get-tuple-element.28), channel_id=1, replica_groups=mesh['band'=8,'pw'=64] {'pw'}, dimensions={0} | all-to-all | bytes 196608 | tf_op jit(solution)/shard_map/all_to_all | solution.py:707
  47.9 0.0 copy-done.5
  47.9 0.0 copy-done.6
  47.9 10.0 %shard_map.166 = (f32[64,3,128]{2,1,0:T(4,128)S(1)}, bf16[8,1024,256]{2,1,0:T(8,128)(2,1)S(1)}) custom-call(s32[24,256]{1,0:T(8,128)S(1)} %copy-done.4, f32[3,208,256]{2,1,0:T(8,128)S(1)} %get-tuple-element.26.refs_1_, bf16[208,624]{1,0:T(8,128)(2,1)S(1)} %copy-done.6, bf16[768,256]{1,0:T(8,128)(2,1)S(1)} %copy-done.5, ...), custom_call_target="tpu_custom_call" | custom-call | flops 1000000 | bytes 4000000 | tf_op jit(solution)/shard_map/pallas_call | solution.py:96
  57.9 14.9 %all_to_all.31.refs_7_ = f32[64,3,128]{2,1,0:T(4,128)S(1)} all-to-all(f32[64,3,128]{2,1,0:T(4,128)S(1)} %get-tuple-element.30), channel_id=1, replica_groups=mesh['band'=8,'pw'=64] {'pw'}, dimensions={0} | all-to-all | bytes 196608 | tf_op jit(solution)/shard_map/all_to_all | solution.py:707
  72.8 0.0 copy-done.8
  72.8 0.0 copy-done.9
  72.8 1.2 %shard_map.167 = f32[8,8,128]{2,1,0:T(8,128)S(1)} custom-call(s32[24,256]{1,0:T(8,128)S(1)} %copy-done.4, f32[8,8,256]{2,1,0:T(8,128)S(1)} %copy-done.7, f32[8,256]{1,0:T(8,128)S(1)} %copy-done.8, f32[1,8]{1,0:T(1,128)S(1)} %bitcast.8, bf16[8,1024,256]{2,1,0:T(8,128)(2,1)S(1)} %get-tuple-element.29.refs_4_, bf16[4,192,192]{2,1,0:T(8,128)(2,1)S(1)} %copy-done, ...), custom_call_target="tpu_custom_call" | custom-call | flops 1000000 | bytes 4000000 | tf_op jit(solution)/shard_map/pallas_call | solution.py:96
  74.0 10.6 %all_to_all.32.refs_1_ = f32[8,8,128]{2,1,0:T(8,128)S(1)} all-to-all(f32[8,8,128]{2,1,0:T(8,128)S(1)} %shard_map.167), channel_id=1, replica_groups=mesh['band'=8,'pw'=64] {'band'}, dimensions={0} | all-to-all | bytes 65536 | tf_op jit(solution)/shard_map/all_to_all | solution.py:707
  84.7 0.0 copy-done.2
  84.7 0.5 shard_map.168
  85.2 10.1 %all_to_all.33.got_ref = f32[16,1,1152]{2,1,0:T(1,128)S(1)} all-to-all(f32[16,1,1152]{2,1,0:T(1,128)S(1)} %get-tuple-element.33), channel_id=1, replica_groups={{0,1,2,3,4,5,6,7,64,65,66,67,68,69,70,71},{8,9,10,11,12,13,14,15,72,73,..., dimensions={0} | all-to-all | bytes 147456 | tf_op jit(solution)/shard_map/all_to_all | solution.py:707
  95.4 14.6 %all_to_all.34.got_ref = f32[32,1,1152]{2,1,0:T(1,128)S(1)} all-to-all(f32[32,1,1152]{2,1,0:T(1,128)S(1)} %shard_map.169), channel_id=1, replica_groups={{0,8,16,24,32,40,48,56,128,136,144,152,160,168,176,184,256,264,272,280,..., dimensions={0} | all-to-all | bytes 294912 | tf_op jit(solution)/shard_map/all_to_all | solution.py:707
  110.0 1.9 %shard_map.170 = (f32[16,128]{1,0:T(8,128)}, f32[16,128]{1,0:T(8,128)}, f32[64,8]{1,0:T(8,128)}, f32[64,8]{1,0:T(8,128)}, f32[8,8]{1,0:T(8,128)}, /*index=5*/f32[8,8]{1,0:T(8,128)}) custom-call(f32[128,256]{1,0:T(8,128)S(1)} %copy-done.2, f32[16,256]{1,0:T(8,128)S(1)} %get-tuple-element.31.image_ref, f32[128,128]{1,0:T(8,128)S(1)} %get-tuple-element.32.over_ref, ...), custom_call_target="tpu_custom_call" | custom-call | flops 1000000 | bytes 4000000 | tf_op jit(solution)/shard_map/pallas_call | solution.py:96
  (3 shorter events, 0.0 us)
Async XLA Ops:
  0.6 19.9 %copy-start = (bf16[4,192,192]{2,1,0:T(8,128)(2,1)S(1)}, bf16[4,192,192]{2,1,0:T(8,128)(2,1)}, u32[]{:S(2)}) copy-start(bf16[4,192,192]{2,1,0:T(8,128)(2,1)} %constant.6.clone.refs_3_.refs_5_) | copy-start | bytes 884740
  0.6 19.9 %copy-start.1 = (f32[3,192,192]{2,1,0:T(8,128)S(1)}, f32[3,192,192]{2,1,0:T(8,128)}, u32[]{:S(2)}) copy-start(f32[3,192,192]{2,1,0:T(8,128)} %refs_4_.1) | copy-start | bytes 1327108
  2.8 17.8 %all-to-all-start = ((f32[8,8,128]{2,1,0:T(8,128)}), f32[8,8,128]{2,1,0:T(8,128)S(1)}, u32[]{:S(2)}, u32[]{:S(2)}) async-start(f32[8,8,128]{2,1,0:T(8,128)} %get-tuple-element.25), calls=%async_computation | async-start | bytes 65536 | tf_op jit(solution)/shard_map/all_to_all | solution.py:707
  13.7 0.7 copy-start.3
  14.4 6.1 %copy-start.4 = (s32[24,256]{1,0:T(8,128)S(1)}, s32[24,256]{1,0:T(8,128)}, u32[]{:S(2)}) copy-start(s32[24,256]{1,0:T(8,128)} %get-tuple-element.24.refs_0_) | copy-start | bytes 73732
  14.4 6.2 %copy-start.7 = (f32[8,8,256]{2,1,0:T(8,128)S(1)}, f32[8,8,256]{2,1,0:T(8,128)}, u32[]{:S(2)}) copy-start(f32[8,8,256]{2,1,0:T(8,128)} %refs_1_.3) | copy-start | bytes 196612
  14.4 33.5 %copy-start.5 = (bf16[768,256]{1,0:T(8,128)(2,1)S(1)}, bf16[768,256]{1,0:T(8,128)(2,1)}, u32[]{:S(2)}) copy-start(bf16[768,256]{1,0:T(8,128)(2,1)} %constant.8.clone.refs_3_) | copy-start | bytes 1179652
  14.4 33.5 %copy-start.6 = (bf16[208,624]{1,0:T(8,128)(2,1)S(1)}, bf16[208,624]{1,0:T(8,128)(2,1)}, u32[]{:S(2)}) copy-start(bf16[208,624]{1,0:T(8,128)(2,1)} %constant.7.clone.refs_2_) | copy-start | bytes 778756
  18.6 54.3 %copy-start.8 = (f32[8,256]{1,0:T(8,128)S(1)}, f32[8,256]{1,0:T(8,128)}, u32[]{:S(2)}) copy-start(f32[8,256]{1,0:T(8,128)} %refs_2_.2) | copy-start | bytes 24580
  18.6 54.2 %copy-start.9 = (f32[8]{0:T(128)S(1)}, f32[8]{0:T(128)}, u32[]{:S(2)}) copy-start(f32[8]{0:T(128)} %param.17) | copy-start | bytes 100
  18.6 66.1 %copy-start.2 = (f32[128,256]{1,0:T(8,128)S(1)}, f32[128,256]{1,0:T(8,128)}, u32[]{:S(2)}) copy-start(f32[128,256]{1,0:T(8,128)} %get-tuple-element.23.refs_0_.basis_ref) | copy-start | bytes 393220
